TPU v7x, 256 devices: a whole 4x4x8 slice. The times are simulated.
256 devices in a mesh: grp: 4 (over y), tile: 64 (over z, x, core).
Axes of the slice: x: 4, y: 4, z: 8, core: 2. Of those that a mesh axis runs over, the one named last changes fastest.
Arguments:
- pieces: bfloat16 [16384, 128, 128], P(('grp', 'tile')), may hold values from -6 to 6
- row_taps: bfloat16 [21, 41], replicated, may hold values from -1 to 1
- col_taps: bfloat16 [21, 41], replicated, may hold values from -1 to 1
- coeffs: float32 [16384, 21], P(('grp', 'tile')), may hold values from -1.25 to 1.25
- weights: bfloat16 [16384], P(('grp', 'tile')), may hold values from 0.25 to 4
- blocks: int32 [16384], P(('grp', 'tile')), may hold values from 0 to 15
- routes: int32 [16384, 1], P(('grp', 'tile')), may hold values from 0 to 63; in each aligned block of 64 rows (0 to 63, 64 to 127, ...) at most 2 rows name the same one
Outputs:
- difference: bfloat16 [16384, 128, 128], P(('grp', 'tile'))
- coadd: bfloat16 [1024, 16384], P('tile')
Inputs may be any that keep to these rules, and one draw needn't show every extreme that they name: `routes`: in the rows of one device no owner is named more than 2 times, a bound that some block reaches.
All inputs are finite; a program needn't handle non-finite values.
Results may differ from a plain program's by a relative error of at most 0.0059.
Values may be sent and summed in bfloat16 or wider, within the bound.
No kernel may reach another device: no remote copies, remote signals or barrier semaphores. Data moves between devices by JAX's collectives and lax.ppermute only.
A program may use at most 64 MiB of HBM per device.

v0:
```python
import jax
import jax.numpy as jnp
from jax import lax
from jax.sharding import PartitionSpec as P

BLOCKS = 16


def toeplitz(taps, side):
    width = taps.shape[1]
    half = (width - 1) // 2
    rows = jnp.arange(side, dtype=jnp.int32)
    offset = rows[None, :] - rows[:, None] + half
    marks = (offset[:, :, None] == jnp.arange(width, dtype=jnp.int32)[None, None, :]).astype(
        jnp.float32
    )
    return jnp.einsum("imk,bk->bim", marks, taps.astype(jnp.float32)).astype(jnp.bfloat16)


def convolve_group(blocks_in, coef, row_mats, col_mats):
    inner = jnp.einsum("pim,bjm->pbij", blocks_in, col_mats, preferred_element_type=jnp.float32)
    inner = (inner * coef[:, :, None, None]).astype(jnp.bfloat16)
    outer = jnp.einsum("bim,pbmj->pij", row_mats, inner, preferred_element_type=jnp.float32)
    return outer.astype(jnp.bfloat16)


def body(pieces, row_taps, col_taps, coeffs, weights, blocks, routes):
    count = pieces.shape[0]
    side = pieces.shape[1]
    owners = lax.axis_size("tile")
    capacity = max(2, 2 * count // owners)
    slots = owners * capacity
    row_mats = toeplitz(row_taps, side)
    col_mats = toeplitz(col_taps, side)
    group = min(8, count)
    grouped = pieces.reshape(count // group, group, side, side)
    coef_grouped = coeffs.reshape(count // group, group, coeffs.shape[1])
    matched = lax.map(
        lambda item: convolve_group(item[0], item[1], row_mats, col_mats), (grouped, coef_grouped)
    )
    matched = matched.reshape(count, side * side)
    owner = routes[:, 0]
    order = jnp.arange(count, dtype=jnp.int32)
    same_owner = owner[:, None] == owner[None, :]
    earlier = order[None, :] < order[:, None]
    rank = jnp.sum(jnp.logical_and(same_owner, earlier).astype(jnp.int32), axis=1)
    slot_of = owner * capacity + rank
    select = (jnp.arange(slots, dtype=jnp.int32)[:, None] == slot_of[None, :]).astype(jnp.bfloat16)
    marked = jnp.where(
        blocks[:, None] == jnp.arange(BLOCKS, dtype=jnp.int32)[None, :],
        weights[:, None],
        jnp.zeros((), jnp.bfloat16),
    )
    sent = jnp.dot(select, matched, preferred_element_type=jnp.float32).astype(jnp.bfloat16)
    sent_marks = jnp.dot(select, marked, preferred_element_type=jnp.float32).astype(jnp.bfloat16)
    received, marks = (
        lax.all_to_all(sent, "tile", split_axis=0, concat_axis=0, tiled=True),
        lax.all_to_all(sent_marks, "tile", split_axis=0, concat_axis=0, tiled=True),
    )
    numer = jnp.dot(marks.T, received, preferred_element_type=jnp.float32)
    wsum = jnp.sum(marks.astype(jnp.float32), axis=0)
    numer_all, wsum_all = lax.psum((numer, wsum), "grp")
    coadd = (numer_all / jnp.maximum(wsum_all, 1.0)[:, None]).astype(jnp.bfloat16)
    present = (marks != 0).astype(jnp.bfloat16)
    cutouts = jnp.dot(present, coadd, preferred_element_type=jnp.float32).astype(jnp.bfloat16)
    returned = lax.all_to_all(cutouts, "tile", split_axis=0, concat_axis=0, tiled=True)
    under = jnp.dot(select.T, returned, preferred_element_type=jnp.float32)
    difference = (matched.astype(jnp.float32) - under).astype(jnp.bfloat16)
    return (difference.reshape(count, side, side), coadd)


def solution(mesh):
    in_specs = (
        P(("grp", "tile"), None, None),
        P(),
        P(),
        P(("grp", "tile"), None),
        P(("grp", "tile")),
        P(("grp", "tile")),
        P(("grp", "tile"), None),
    )
    out_specs = (P(("grp", "tile"), None, None), P("tile", None))
    return jax.shard_map(body, mesh=mesh, in_specs=in_specs, out_specs=out_specs, check_vma=False)
```

profile of v0, /device:TPU:1, one launch (start us, length us, event | category | flops | bytes accessed | tf_op | source)
XLA Modules:
  0.0 371.4 jit_solution(15718441248233897111)
XLA Ops:
  7.2 0.9 convert_reduce_fusion.1
  8.1 0.7 multiply_add_fusion
  8.8 0.9 convolution_convert_fusion.2
  9.7 0.7 copy.36
  10.4 13.0 %all-to-all-start = ((bf16[64,2,16]{2,1,0:T(2,128)(2,1)}), bf16[64,2,16]{2,1,0:T(2,128)(2,1)S(1)}, u32[]{:S(2)}, u32[]{:S(2)}) async-start(bf16[64,2,16]{2,1,0:T(2,128)(2,1)} %bitcast.19), calls=%async_computation | async-start | bytes 65536 | tf_op jit(solution)/shard_map/all_to_all | solution.py:58
  23.5 0.8 copy.32
  24.3 0.7 fusion.34
  25.2 1.4 fusion.35
  26.6 1.0 copy.33
  27.6 37.0 %while.10 = (s32[]{:T(128)}, bf16[8,8,128,128]{3,1,2,0:T(8,128)(2,1)S(1)}, bf16[8,8,128,128]{3,2,1,0:T(8,128)(2,1)}, bf16[21,128,128]{2,1,0:T(8,128)(2,1)}, f32[...) while((s32[]{:T(128)}, bf16[8,8,128,128]{3,1,2,0:T(8,128)(2,1)S(1)}, ...), condition=%wide.region_1.2_spmd, body=%wide.region_0.1_spmd.sunk | while | flops 1414922240 | bytes 2951233 | solution.py:38
  27.6 4.3 %fusion.61 = bf16[1,8,128,128]{2,3,1,0:T(8,128)(2,1)S(1)} fusion(f32[8,21]{1,0:T(8,128)S(1)} %dynamic-slice_bitcast_fusion.2, bf16[21,128,128]{2,1,0:T(8,128)(2,1)S(1)} %get-tuple-element.127, bf16[21,128,128]{2,1,0:T(8,128)(2,1)} %get-tuple-element.125, bf16[8,8,128,128]{3,2,1,0:T(8,128)(2,1)} %get-tuple-element.124, s32[]{:T(128)S(6)} %copy.54), kind=kOutput, calls=%fused_computation.7.clone.1 | convolution fusion | flops 1414922240 | bytes 1901220 | tf_op jit(solution)/shard_map/while/body/eval_jaxpr/bim,pbmj->pij/dot_general | solution.py:23
  32.2 4.3 %fusion.61 = bf16[1,8,128,128]{2,3,1,0:T(8,128)(2,1)S(1)} fusion(f32[8,21]{1,0:T(8,128)S(1)} %dynamic-slice_bitcast_fusion.2, bf16[21,128,128]{2,1,0:T(8,128)(2,1)S(1)} %get-tuple-element.127, bf16[21,128,128]{2,1,0:T(8,128)(2,1)} %get-tuple-element.125, bf16[8,8,128,128]{3,2,1,0:T(8,128)(2,1)} %get-tuple-element.124, s32[]{:T(128)S(6)} %copy.54), kind=kOutput, calls=%fused_computation.7.clone.1 | convolution fusion | flops 1414922240 | bytes 1901220 | tf_op jit(solution)/shard_map/while/body/eval_jaxpr/bim,pbmj->pij/dot_general | solution.py:23
  36.6 0.2 copy.50
  36.8 4.3 %fusion.61 = bf16[1,8,128,128]{2,3,1,0:T(8,128)(2,1)S(1)} fusion(f32[8,21]{1,0:T(8,128)S(1)} %dynamic-slice_bitcast_fusion.2, bf16[21,128,128]{2,1,0:T(8,128)(2,1)S(1)} %get-tuple-element.127, bf16[21,128,128]{2,1,0:T(8,128)(2,1)} %get-tuple-element.125, bf16[8,8,128,128]{3,2,1,0:T(8,128)(2,1)} %get-tuple-element.124, s32[]{:T(128)S(6)} %copy.54), kind=kOutput, calls=%fused_computation.7.clone.1 | convolution fusion | flops 1414922240 | bytes 1901220 | tf_op jit(solution)/shard_map/while/body/eval_jaxpr/bim,pbmj->pij/dot_general | solution.py:23
  41.5 4.3 %fusion.61 = bf16[1,8,128,128]{2,3,1,0:T(8,128)(2,1)S(1)} fusion(f32[8,21]{1,0:T(8,128)S(1)} %dynamic-slice_bitcast_fusion.2, bf16[21,128,128]{2,1,0:T(8,128)(2,1)S(1)} %get-tuple-element.127, bf16[21,128,128]{2,1,0:T(8,128)(2,1)} %get-tuple-element.125, bf16[8,8,128,128]{3,2,1,0:T(8,128)(2,1)} %get-tuple-element.124, s32[]{:T(128)S(6)} %copy.54), kind=kOutput, calls=%fused_computation.7.clone.1 | convolution fusion | flops 1414922240 | bytes 1901220 | tf_op jit(solution)/shard_map/while/body/eval_jaxpr/bim,pbmj->pij/dot_general | solution.py:23
  46.1 4.3 %fusion.61 = bf16[1,8,128,128]{2,3,1,0:T(8,128)(2,1)S(1)} fusion(f32[8,21]{1,0:T(8,128)S(1)} %dynamic-slice_bitcast_fusion.2, bf16[21,128,128]{2,1,0:T(8,128)(2,1)S(1)} %get-tuple-element.127, bf16[21,128,128]{2,1,0:T(8,128)(2,1)} %get-tuple-element.125, bf16[8,8,128,128]{3,2,1,0:T(8,128)(2,1)} %get-tuple-element.124, s32[]{:T(128)S(6)} %copy.54), kind=kOutput, calls=%fused_computation.7.clone.1 | convolution fusion | flops 1414922240 | bytes 1901220 | tf_op jit(solution)/shard_map/while/body/eval_jaxpr/bim,pbmj->pij/dot_general | solution.py:23
  50.7 4.3 %fusion.61 = bf16[1,8,128,128]{2,3,1,0:T(8,128)(2,1)S(1)} fusion(f32[8,21]{1,0:T(8,128)S(1)} %dynamic-slice_bitcast_fusion.2, bf16[21,128,128]{2,1,0:T(8,128)(2,1)S(1)} %get-tuple-element.127, bf16[21,128,128]{2,1,0:T(8,128)(2,1)} %get-tuple-element.125, bf16[8,8,128,128]{3,2,1,0:T(8,128)(2,1)} %get-tuple-element.124, s32[]{:T(128)S(6)} %copy.54), kind=kOutput, calls=%fused_computation.7.clone.1 | convolution fusion | flops 1414922240 | bytes 1901220 | tf_op jit(solution)/shard_map/while/body/eval_jaxpr/bim,pbmj->pij/dot_general | solution.py:23
  55.4 4.3 %fusion.61 = bf16[1,8,128,128]{2,3,1,0:T(8,128)(2,1)S(1)} fusion(f32[8,21]{1,0:T(8,128)S(1)} %dynamic-slice_bitcast_fusion.2, bf16[21,128,128]{2,1,0:T(8,128)(2,1)S(1)} %get-tuple-element.127, bf16[21,128,128]{2,1,0:T(8,128)(2,1)} %get-tuple-element.125, bf16[8,8,128,128]{3,2,1,0:T(8,128)(2,1)} %get-tuple-element.124, s32[]{:T(128)S(6)} %copy.54), kind=kOutput, calls=%fused_computation.7.clone.1 | convolution fusion | flops 1414922240 | bytes 1901220 | tf_op jit(solution)/shard_map/while/body/eval_jaxpr/bim,pbmj->pij/dot_general | solution.py:23
  60.0 4.3 %fusion.61 = bf16[1,8,128,128]{2,3,1,0:T(8,128)(2,1)S(1)} fusion(f32[8,21]{1,0:T(8,128)S(1)} %dynamic-slice_bitcast_fusion.2, bf16[21,128,128]{2,1,0:T(8,128)(2,1)S(1)} %get-tuple-element.127, bf16[21,128,128]{2,1,0:T(8,128)(2,1)} %get-tuple-element.125, bf16[8,8,128,128]{3,2,1,0:T(8,128)(2,1)} %get-tuple-element.124, s32[]{:T(128)S(6)} %copy.54), kind=kOutput, calls=%fused_computation.7.clone.1 | convolution fusion | flops 1414922240 | bytes 1901220 | tf_op jit(solution)/shard_map/while/body/eval_jaxpr/bim,pbmj->pij/dot_general | solution.py:23
  64.6 3.2 convolution_convert_fusion.1
  67.8 7.6 %all_to_all.22 = bf16[64,2,16384]{2,1,0:T(2,128)(2,1)} reshape(bf16[128,16384]{1,0:T(8,128)(2,1)} %convolution_convert_fusion.1) | data formatting | bytes 8388608 | tf_op jit(solution)/shard_map/all_to_all | solution.py:57
  75.4 104.9 %all_to_all.30 = bf16[64,2,16384]{2,1,0:T(2,128)(2,1)S(1)} all-to-all(bf16[64,2,16384]{2,1,0:T(2,128)(2,1)} %all_to_all.22), channel_id=1, replica_groups=mesh['grp'=4,'tile'=64] {'tile'}, dimensions={0} | all-to-all | bytes 8388608 | tf_op jit(solution)/shard_map/all_to_all | solution.py:57
  180.3 5.5 %convolution_bitcast_fusion = f32[16,16384]{1,0:T(8,128)} fusion(bf16[64,2,16384]{2,1,0:T(2,128)(2,1)S(1)} %all_to_all.30, bf16[64,2,16]{2,1,0:T(2,128)(2,1)S(1)} %all-to-all-done), kind=kOutput, calls=%fused_computation.19 | convolution fusion | flops 67108864 | bytes 5246976 | tf_op jit(solution)/shard_map/dot_general | solution.py:60
  186.0 8.7 %psum.15 = f32[16]{0:T(128)S(1)} all-reduce(f32[16]{0:T(128)S(1)} %convert_reduce_fusion), channel_id=1, replica_groups=mesh['grp'=4,'tile'=64] {'grp'}, use_global_device_ids=true, to_apply=%region_5.6 | all-reduce | flops 16 | bytes 128 | tf_op jit(solution)/shard_map/psum | solution.py:62
  194.7 38.6 %all-reduce.2.cloned.1.call-done = f32[16,16384]{1,0:T(8,128)} async-done(((f32[16,16384]{1,0:T(8,128)}), f32[16,16384]{1,0:T(8,128)}) %all-reduce.2.cloned.1.call-update) | async-done | bytes 1048592 | tf_op jit(solution)/shard_map/psum | solution.py:62
  233.3 1.4 divide_convert_fusion
  234.7 3.2 convolution_convert_fusion
  237.9 7.6 %all_to_all.24 = bf16[64,2,16384]{2,1,0:T(2,128)(2,1)} reshape(bf16[128,16384]{1,0:T(8,128)(2,1)} %convolution_convert_fusion) | data formatting | bytes 8388608 | tf_op jit(solution)/shard_map/all_to_all | solution.py:66
  245.5 106.8 %all_to_all.31 = bf16[64,2,16384]{2,1,0:T(2,128)(2,1)} all-to-all(bf16[64,2,16384]{2,1,0:T(2,128)(2,1)} %all_to_all.24), channel_id=1, replica_groups=mesh['grp'=4,'tile'=64] {'tile'}, dimensions={0} | all-to-all | bytes 8388608 | tf_op jit(solution)/shard_map/all_to_all | solution.py:66
  352.3 7.2 %all_to_all.26 = bf16[128,16384]{1,0:T(8,128)(2,1)} reshape(bf16[64,2,16384]{2,1,0:T(2,128)(2,1)} %all_to_all.31) | data formatting | bytes 8388608 | tf_op jit(solution)/shard_map/all_to_all | solution.py:66
  359.5 3.1 fusion.29
  362.6 1.9 copy.44
  (37 shorter events, 2.1 us)
Async XLA Ops:
  7.2 17.1 %copy-start = (bf16[21,41]{1,0:T(8,128)(2,1)S(1)}, bf16[21,41]{1,0:T(8,128)(2,1)}, u32[]{:S(2)}) copy-start(bf16[21,41]{1,0:T(8,128)(2,1)} %param.10) | copy-start | bytes 5170
  10.4 65.0 %all-to-all-start = ((bf16[64,2,16]{2,1,0:T(2,128)(2,1)}), bf16[64,2,16]{2,1,0:T(2,128)(2,1)S(1)}, u32[]{:S(2)}, u32[]{:S(2)}) async-start(bf16[64,2,16]{2,1,0:T(2,128)(2,1)} %bitcast.19), calls=%async_computation | async-start | bytes 65536 | tf_op jit(solution)/shard_map/all_to_all | solution.py:58
  23.4 209.9 %all-reduce.2.cloned.1.call-start = ((), (), s32[]{:S(2)}) async-start(), calls=%async_computation.3 | async-start | bytes 2097152 | tf_op jit(solution)/shard_map/psum | solution.py:62
  234.7 10.8 %copy-start.1 = (bf16[16,16384]{1,0:T(8,128)(2,1)}, bf16[16,16384]{1,0:T(8,128)(2,1)S(1)}, u32[]{:S(2)}) copy-start(bf16[16,16384]{1,0:T(8,128)(2,1)S(1)} %divide_convert_fusion) | copy-start | bytes 1572868
Sparse Core Ops, SparseCore 0:
  185.9 47.3 all-reduce.1
where the time goes:
time: 373 us; the launch traced here: 371 us
  blocking collectives  220 us (59%)
  matrix products  52.8 us (14%)
  waiting for transfers between devices  38.7 us (10%)
  local copies, waits for them, and re-layouts  29 us (8%)
  between operations  14.1 us (4%)
  starting transfers between devices  13 us (3%)
    all_to_all x1, blocking collectives, body(): lax.all_to_all(cutouts, 'tile', split_axis=0, concat_axis=0, tiled=True)  107 us
    all_to_all x1, blocking collectives, body(): lax.all_to_all(sent, 'tile', split_axis=0, concat_axis=0, tiled=True)  105 us
    psum x1, waiting for transfers between devices, body(): numer_all, wsum_all = lax.psum((numer, wsum), 'grp')  38.6 us
    dot_general x8, matrix products, convolve_group(): jnp.einsum('bim,pbmj->pij', row_mats, inner, preferred_element_type=jnp.f...  34.8 us
    all_to_all x2, local copies, waits for them, and re-layouts, body(): lax.all_to_all(cutouts, 'tile', split_axis=0, concat_axis=0, tiled=True)  14.8 us
    all_to_all x1, starting transfers between devices, body(): lax.all_to_all(sent_marks, 'tile', split_axis=0, concat_axis=0, tiled=True)  13 us
    psum x1, blocking collectives, body(): numer_all, wsum_all = lax.psum((numer, wsum), 'grp')  8.72 us
    all_to_all x1, local copies, waits for them, and re-layouts, body(): lax.all_to_all(sent, 'tile', split_axis=0, concat_axis=0, tiled=True)  7.62 us
  transfers between devices with their start and end apart: 2, of which 1 were waited for; matrix products, arithmetic and copies ran while one was open for 12% of the time, Pallas kernels for 0%

commit v1 on v0

v1 whole, which is shorter than its diff:
```python
import functools

import jax
import jax.numpy as jnp
from jax import lax
from jax.experimental import pallas as pl
from jax.experimental.pallas import tpu as pltpu
from jax.sharding import Mesh, PartitionSpec as P

BLOCKS = 16
SIDE = 128
GROUP = 16
HEAD = 8
TAIL = 16
FAR = "far"
PLANE = ("y", "near", "x", "c")
EVERY = ("y", "far", "near", "x", "c")
BF16 = jnp.bfloat16
F32 = jnp.float32


def params(limit=56 << 20):
    return pltpu.CompilerParams(vmem_limit_bytes=limit)


def cost(flops, nbytes):
    return pl.CostEstimate(flops=flops, bytes_accessed=nbytes, transcendentals=0)


def band(taps_ref, b, half):
    line = jnp.broadcast_to(taps_ref[b : b + 1, :], (SIDE, SIDE))
    moved = pltpu.roll(line, 0, 1, stride=1, stride_axis=0)
    rows = lax.broadcasted_iota(jnp.int32, (SIDE, SIDE), 0)
    columns = lax.broadcasted_iota(jnp.int32, (SIDE, SIDE), 1)
    return jnp.where(jnp.abs(columns - rows) <= half, moved, 0.0)


def conv_kernel(nb, half, coef_ref, x_ref, col_taps_ref, row_taps_ref, out_ref, col_ref, row_ref, taps_ref, z_ref, m_ref):
    step = pl.program_id(0)

    @pl.when(step == 0)
    def _():
        for source, target, flip in ((col_taps_ref, col_ref, True), (row_taps_ref, row_ref, False)):
            taps_ref[...] = jnp.zeros_like(taps_ref)
            taps_ref[:nb, : 2 * half + 1] = source[...].astype(F32)
            taps_ref[...] = pltpu.roll(taps_ref[...], SIDE - half, 1)
            for b in range(nb):
                matrix = band(taps_ref, b, half)
                matrix = matrix.T if flip else matrix
                target[:, b * SIDE : (b + 1) * SIDE] = matrix.astype(BF16)

    x = x_ref[...].reshape(GROUP * SIDE, SIDE)
    for first in range(0, nb, 2):
        some = min(2, nb - first)
        inner = jnp.dot(x, col_ref[:, first * SIDE : (first + some) * SIDE], preferred_element_type=F32)
        for k in range(some):
            b = first + k
            for p in range(GROUP):
                part = inner[p * SIDE : (p + 1) * SIDE, k * SIDE : (k + 1) * SIDE]
                z_ref[p // 2, b * SIDE : (b + 1) * SIDE, (p % 2) * SIDE : (p % 2 + 1) * SIDE] = (
                    part * coef_ref[step * GROUP + p, b]
                ).astype(BF16)
    for pair in range(GROUP // 2):
        outer = jnp.dot(row_ref[...], z_ref[pair], preferred_element_type=F32)
        m_ref[2 * pair * SIDE : (2 * pair + 1) * SIDE] = outer[:, :SIDE]
        m_ref[(2 * pair + 1) * SIDE : (2 * pair + 2) * SIDE] = outer[:, SIDE:]
    per = SIDE // out_ref.shape[0]
    for i in range(SIDE):
        t, k = divmod(i, per)
        out_ref[t, :, k * SIDE : (k + 1) * SIDE] = m_ref[pl.ds(i, GROUP, stride=SIDE), :].astype(BF16)


def convolve(pieces, coeffs, col_taps, row_taps, chunks):
    count = pieces.shape[0]
    nb, width = row_taps.shape
    padded = -(-nb // 8) * 8
    return pl.pallas_call(
        functools.partial(conv_kernel, nb, (width - 1) // 2),
        grid=(count // GROUP,),
        in_specs=[
            pl.BlockSpec(memory_space=pltpu.SMEM),
            pl.BlockSpec((GROUP, SIDE, SIDE), lambda g: (g, 0, 0)),
            pl.BlockSpec((nb, width), lambda g: (0, 0)),
            pl.BlockSpec((nb, width), lambda g: (0, 0)),
        ],
        out_specs=pl.BlockSpec((chunks, GROUP, SIDE * SIDE // chunks), lambda g: (0, g, 0)),
        out_shape=jax.ShapeDtypeStruct((chunks, count, SIDE * SIDE // chunks), BF16),
        scratch_shapes=[
            pltpu.VMEM((SIDE, nb * SIDE), BF16),
            pltpu.VMEM((SIDE, nb * SIDE), BF16),
            pltpu.VMEM((padded, SIDE), F32),
            pltpu.VMEM((GROUP // 2, nb * SIDE, 2 * SIDE), BF16),
            pltpu.VMEM((GROUP * SIDE, SIDE), F32),
        ],
        compiler_params=params(),
        cost_estimate=cost(count * nb * SIDE**3 * 4, count * SIDE * SIDE * 4),
        name="convolve",
    )(coeffs, pieces, col_taps, row_taps)


def partial_kernel(steps, own_rows, z_ref, info_ref, got_ref, *refs):
    outs, (row_ref, weight_ref) = refs[:steps], refs[steps:]
    sources = info_ref.shape[0]
    left = lax.broadcasted_iota(jnp.int32, (1, SIDE), 1) < SIDE // 2
    for a in range(sources // 2):
        for line, target in ((0, row_ref), (1, weight_ref)):
            both = jnp.where(left, info_ref[2 * a, line : line + 1, :], info_ref[2 * a + 1, line : line + 1, :])
            target[:, a * SIDE : (a + 1) * SIDE] = both
    row = row_ref[...].astype(jnp.int32)
    weight = weight_ref[...]
    index = lax.broadcasted_iota(jnp.int32, (own_rows, row.shape[1]), 0)
    for k in range(steps):
        first = lax.rem(z_ref[0] + k, steps) * own_rows
        marks = jnp.where(index == row - first, weight, 0.0)
        part = jnp.dot(marks.astype(BF16), got_ref[...], preferred_element_type=F32)
        outs[k][:own_rows, :] = part.astype(BF16)
        total = jnp.broadcast_to(jnp.sum(marks, axis=1, keepdims=True), (own_rows, SIDE)).T[:TAIL]
        high = total.astype(BF16).astype(F32)
        middle = (total - high).astype(BF16).astype(F32)
        low = total - high - middle
        line = lax.broadcasted_iota(jnp.int32, total.shape, 0)
        terms = jnp.where(line == 0, high, jnp.where(line == 1, middle, jnp.where(line == 2, low, 0.0)))
        outs[k][own_rows:, :] = terms.astype(BF16)


def partial_sums(z, info, got, steps, own_rows):
    held, width = got.shape
    vmem = pl.BlockSpec(memory_space=pltpu.VMEM)
    return pl.pallas_call(
        functools.partial(partial_kernel, steps, own_rows),
        in_specs=[pl.BlockSpec(memory_space=pltpu.SMEM), vmem, vmem],
        out_specs=[vmem] * steps,
        out_shape=[jax.ShapeDtypeStruct((own_rows + TAIL, width), BF16)] * steps,
        scratch_shapes=[pltpu.VMEM((1, held), F32), pltpu.VMEM((1, held), F32)],
        compiler_params=params(),
        cost_estimate=cost(2 * steps * own_rows * held * width, (held + steps * own_rows) * width * 2),
        name="partial_sums",
    )(z, info, got)


def average_kernel(own_rows, *refs):
    parts, out_ref = refs[:-1], refs[-1]
    terms = sum(ref[own_rows:, :].astype(F32) for ref in parts)
    line = jnp.sum(terms, axis=0, keepdims=True)
    below = jnp.maximum(jnp.broadcast_to(line, (SIDE, own_rows)).T, 1.0)
    total = sum(ref[:own_rows, :].astype(F32) for ref in parts)
    for k in range(total.shape[1] // SIDE):
        span = slice(k * SIDE, (k + 1) * SIDE)
        out_ref[:, span] = (total[:, span] / below).astype(BF16)


def average(parts, own_rows):
    width = parts[0].shape[1]
    vmem = pl.BlockSpec(memory_space=pltpu.VMEM)
    return pl.pallas_call(
        functools.partial(average_kernel, own_rows),
        in_specs=[vmem] * len(parts),
        out_specs=vmem,
        out_shape=jax.ShapeDtypeStruct((own_rows, width), BF16),
        compiler_params=params(),
        cost_estimate=cost(10 * own_rows * width, 18 * own_rows * width),
        name="average",
    )(*parts)


def subtract_kernel(count, groups, z_ref, info_ref, got_ref, *refs):
    coadds, out_ref, all_ref = refs[:-2], refs[-2], refs[-1]
    steps, own_rows = len(coadds), coadds[0].shape[0]
    total_rows = steps * own_rows
    for k in range(steps):
        all_ref[k * own_rows : (k + 1) * own_rows, :] = coadds[k][...]
    sources = out_ref.shape[0]
    left = lax.broadcasted_iota(jnp.int32, (1, SIDE), 1) < SIDE // 2
    index = lax.broadcasted_iota(jnp.int32, (SIDE, total_rows), 1).astype(F32)
    lanes = min(4, sources // 2)
    for first in range(0, sources // 2, lanes):
        marks = []
        for a in range(first, first + lanes):
            row = jnp.where(left, info_ref[2 * a, :1, :], info_ref[2 * a + 1, :1, :]).astype(jnp.int32)
            back = jnp.bitwise_and(z_ref[0] - jnp.right_shift(row, own_rows.bit_length() - 1) + steps, steps - 1)
            row = back * own_rows + jnp.bitwise_and(row, own_rows - 1)
            column = jnp.broadcast_to(row.astype(F32), (SIDE, SIDE)).T
            column = jnp.concatenate([column] * (total_rows // SIDE), axis=1)
            marks.append(jnp.where(index == column, 1.0, 0.0).astype(BF16))
        under = jnp.dot(jnp.concatenate(marks), all_ref[...], preferred_element_type=F32)
        for a in range(2 * lanes):
            s = 2 * first + a
            piece = got_ref[s * count : (s + 1) * count, :].astype(F32)
            out_ref[s, :count, :] = (piece - under[a * count : (a + 1) * count]).astype(BF16)
            k = s % groups
            out_ref[s, count:, :] = coadds[0][k * BLOCKS : (k + 1) * BLOCKS, :]


def subtract(z, info, got, coadds, count, groups):
    held, width = got.shape
    sources = held // count
    steps, own_rows = len(coadds), coadds[0].shape[0]
    vmem = pl.BlockSpec(memory_space=pltpu.VMEM)
    return pl.pallas_call(
        functools.partial(subtract_kernel, count, groups),
        in_specs=[pl.BlockSpec(memory_space=pltpu.SMEM)] + [vmem] * (2 + steps),
        out_specs=vmem,
        out_shape=jax.ShapeDtypeStruct((sources, count + BLOCKS, width), BF16),
        scratch_shapes=[pltpu.VMEM((steps * own_rows, width), BF16)],
        compiler_params=params(),
        cost_estimate=cost(2 * steps * own_rows * held * width, (2 * held + steps * own_rows) * width * 2),
        name="subtract",
    )(z, info, got, *coadds)


def place_kernel(back_ref, coadd_ref, diff_ref, template_ref, m_ref):
    chunks, _, width = back_ref.shape
    per = width // SIDE
    for t in range(chunks):
        for k in range(per):
            m_ref[pl.ds(t * per + k, GROUP, stride=SIDE), :] = back_ref[
                t, :, k * SIDE : (k + 1) * SIDE
            ].astype(F32)
    diff_ref[...] = m_ref[...].astype(BF16).reshape(diff_ref.shape)
    for t in range(coadd_ref.shape[0]):
        template_ref[:, t * width : (t + 1) * width] = coadd_ref[t]


def place(back, count):
    chunks, _, width = back.shape
    steps = count // GROUP
    some = chunks // steps
    return pl.pallas_call(
        place_kernel,
        grid=(steps,),
        in_specs=[
            pl.BlockSpec((chunks, GROUP, width), lambda g: (0, g, 0)),
            pl.BlockSpec((some, BLOCKS, width), lambda g: (g, count // BLOCKS, 0)),
        ],
        out_specs=(
            pl.BlockSpec((GROUP, SIDE, SIDE), lambda g: (g, 0, 0)),
            pl.BlockSpec((BLOCKS, some * width), lambda g: (0, g)),
        ),
        out_shape=(
            jax.ShapeDtypeStruct((count, SIDE, SIDE), BF16),
            jax.ShapeDtypeStruct((BLOCKS, SIDE * SIDE), BF16),
        ),
        scratch_shapes=[pltpu.VMEM((GROUP * SIDE, SIDE), F32)],
        compiler_params=params(),
        cost_estimate=cost(0, 4 * count * SIDE * SIDE),
        name="place",
    )(back, back)


def shift(array, by, steps):
    return lax.ppermute(array, FAR, [(i, (i + by) % steps) for i in range(steps)])


def body(pieces, row_taps, col_taps, coeffs, weights, blocks, routes):
    count = pieces.shape[0]
    steps = lax.axis_size(FAR)
    chunks = lax.axis_size(PLANE)
    groups = chunks // lax.axis_size("y")
    own_rows = groups * BLOCKS
    z = lax.axis_index(FAR).astype(jnp.int32).reshape(1)

    row = (routes[:, 0] * BLOCKS + blocks).astype(F32)
    info = jnp.stack([jnp.tile(row, 2), jnp.tile(weights.astype(F32), 2)])
    info = jnp.pad(info, ((0, HEAD - 2), (0, 0)))
    info = jnp.broadcast_to(info, (chunks,) + info.shape)
    info = lax.all_to_all(info, PLANE, split_axis=0, concat_axis=0, tiled=True)

    sent = convolve(pieces, coeffs, col_taps, row_taps, chunks)
    got = lax.all_to_all(sent, PLANE, split_axis=0, concat_axis=0, tiled=True)
    got = got.reshape(chunks * count, -1)
    sums = partial_sums(z, info, got, steps, own_rows)
    own = average([sums[0]] + [shift(sums[k], k, steps) for k in range(1, steps)], own_rows)
    coadds = [own] + [shift(own, k, steps) for k in range(1, steps)]
    back = subtract(z, info, got, coadds, count, groups)
    back = lax.all_to_all(back, PLANE, split_axis=0, concat_axis=0, tiled=True)
    return place(back, count)


def solution(mesh):
    finer = Mesh(mesh.devices.reshape(4, 4, 2, 4, 2), EVERY)
    in_specs = (
        P(EVERY, None, None),
        P(),
        P(),
        P(EVERY, None),
        P(EVERY),
        P(EVERY),
        P(EVERY, None),
    )
    out_specs = (P(EVERY, None, None), P(EVERY[1:], None))
    return jax.shard_map(body, mesh=finer, in_specs=in_specs, out_specs=out_specs, check_vma=False)
```

time: 373 us -> 179 us (0.48)
  blocking collectives: 220 us -> 40.6 us
  matrix products: 52.8 us -> 0 us
  Pallas kernels: 0 us -> 43.1 us
  starting transfers between devices: 13 us -> 35.6 us
  local copies, waits for them, and re-layouts: 29 us -> 6.94 us
  between operations: 14.1 us -> 0.68 us
  waiting for transfers between devices: 38.7 us -> 50.8 us
    all_to_all x2 -> x1, blocking collectives: 212 us -> 40.6 us  [body(): back = lax.all_to_all(back, PLANE, split_axis=0, concat_axis=0, tiled=True)]
    dot_general x15 -> x0, matrix products: 52.8 us -> none  [the longest x8 34.8 us: convolve_group(): jnp.einsum('bim,pbmj->pij', row_mats, inner, preferred_element_type=jnp.f...]
    pallas_call x0 -> x5, Pallas kernels: none -> 43.1 us  [the longest x1 23.4 us: convolve(): pl.pallas_call(functools.partial(conv_kernel, nb, (width - 1) // 2), grid...]
    psum x1 -> x0, waiting for transfers between devices: 38.6 us -> none  [body(): numer_all, wsum_all = lax.psum((numer, wsum), 'grp')]
    all_to_all x1 -> x2, waiting for transfers between devices: 0.01 us -> 29 us  [the longest x1 29 us: body(): got = lax.all_to_all(sent, PLANE, split_axis=0, concat_axis=0, tiled=True)]
    all_to_all x3 -> x0, local copies, waits for them, and re-layouts: 22.4 us -> none  [the longest x2 14.8 us: body(): lax.all_to_all(cutouts, 'tile', split_axis=0, concat_axis=0, tiled=True)]
    ppermute x0 -> x6, waiting for transfers between devices: none -> 21.8 us  [shift(): lax.ppermute(array, FAR, [(i, (i + by) % steps) for i in range(steps)])]
    ppermute x0 -> x6, starting transfers between devices: none -> 16.4 us  [shift(): lax.ppermute(array, FAR, [(i, (i + by) % steps) for i in range(steps)])]
  transfers between devices with their start and end apart: 2 -> 8, of which waited for: 1 -> 6; matrix products, arithmetic and copies ran while one was open for 12% -> 1% of each run, Pallas kernels for 0% -> 13%
where the time goes in v1:
time: 179 us; the launch traced here: 178 us
  waiting for transfers between devices  50.8 us (28%)
  Pallas kernels  43.1 us (24%)
  blocking collectives  40.6 us (23%)
  starting transfers between devices  35.6 us (20%)
  local copies, waits for them, and re-layouts  6.94 us (4%)
    all_to_all x1, blocking collectives, body(): back = lax.all_to_all(back, PLANE, split_axis=0, concat_axis=0, tiled=True)  40.6 us
    all_to_all x1, waiting for transfers between devices, body(): got = lax.all_to_all(sent, PLANE, split_axis=0, concat_axis=0, tiled=True)  29 us
    pallas_call x1, Pallas kernels, convolve(): pl.pallas_call(functools.partial(conv_kernel, nb, (width - 1) // 2), grid...  23.4 us
    ppermute x6, waiting for transfers between devices, shift(): lax.ppermute(array, FAR, [(i, (i + by) % steps) for i in range(steps)])  21.8 us
    ppermute x6, starting transfers between devices, shift(): lax.ppermute(array, FAR, [(i, (i + by) % steps) for i in range(steps)])  16.4 us
    all_to_all x1, starting transfers between devices, body(): info = lax.all_to_all(info, PLANE, split_axis=0, concat_axis=0, tiled=True)  10.3 us
    all_to_all x1, starting transfers between devices, body(): got = lax.all_to_all(sent, PLANE, split_axis=0, concat_axis=0, tiled=True)  8.86 us
    pallas_call x1, Pallas kernels, partial_sums(): pl.pallas_call(functools.partial(partial_kernel, steps, own_rows), in_spe...  6.19 us
  transfers between devices with their start and end apart: 8, of which 6 were waited for; matrix products, arithmetic and copies ran while one was open for 1% of the time, Pallas kernels for 13%

profile of v1, /device:TPU:1, one launch (start us, length us, event | category | flops | bytes accessed | tf_op | source)
XLA Modules:
  0.0 178.4 jit_solution(13444141251031259045)
XLA Ops:
  0.6 0.7 fusion
  1.3 0.1 stack_tile.6
  1.4 0.7 tile.5
  2.1 0.1 stack_tile.7
  2.1 0.7 broadcast_in_dim.3
  2.9 10.3 %all-to-all-start = ((f32[64,8,128]{2,1,0:T(8,128)}), f32[64,8,128]{2,1,0:T(8,128)S(1)}, u32[]{:S(2)}, u32[]{:S(2)}) async-start(f32[64,8,128]{2,1,0:T(8,128)} %broadcast_in_dim.3), calls=%async_computation | async-start | bytes 524288 | tf_op jit(solution)/shard_map/all_to_all | solution.py:266
  13.2 1.4 copy.9.coef_ref
  14.6 23.4 %convolve.1 = bf16[64,64,256]{2,1,0:T(8,128)(2,1)} custom-call(f32[64,21]{1,0:T(8,128)} %copy.9.coef_ref, bf16[64,128,128]{2,1,0:T(8,128)(2,1)} %x_ref.1, bf16[21,41]{1,0:T(8,128)(2,1)} %col_taps_ref.1, bf16[21,41]{1,0:T(8,128)(2,1)} %row_taps_ref.1), custom_call_target="tpu_custom_call" | custom-call | flops 11274289152 | bytes 4194304 | tf_op jit(solution)/shard_map/convolve/pallas_call | solution.py:77
  38.1 0.7 copy-done.1
  38.8 8.9 %all-to-all-start.1 = ((bf16[64,64,256]{2,1,0:T(8,128)(2,1)}), bf16[64,64,256]{2,1,0:T(8,128)(2,1)S(1)}, u32[]{:S(2)}, u32[]{:S(2)}) async-start(bf16[64,64,256]{2,1,0:T(8,128)(2,1)} %convolve.1), calls=%async_computation.1 | async-start | bytes 4194304 | tf_op jit(solution)/shard_map/all_to_all | solution.py:269
  47.6 29.0 %all-to-all-done.1 = bf16[64,64,256]{2,1,0:T(8,128)(2,1)S(1)} async-done(((bf16[64,64,256]{2,1,0:T(8,128)(2,1)}), bf16[64,64,256]{2,1,0:T(8,128)(2,1)S(1)}, u32[]{:S(2)}, u32[]{:S(2)}) %all-to-all-start.1) | async-done | bytes 2097184 | tf_op jit(solution)/shard_map/all_to_all | solution.py:269
  76.6 1.3 copy-done
  78.0 6.2 %partial_sums.1 = (bf16[272,256]{1,0:T(8,128)(2,1)}, bf16[272,256]{1,0:T(8,128)(2,1)}, bf16[272,256]{1,0:T(8,128)(2,1)}, bf16[272,256]{1,0:T(8,128)(2,1)}) custom-call(s32[1]{0:T(128)} %bitcast.z_ref, f32[64,8,128]{2,1,0:T(8,128)} %copy-done.1, bf16[4096,256]{1,0:T(8,128)(2,1)} %bitcast.6), custom_call_target="tpu_custom_call" | custom-call | flops 2147483648 | bytes 2621440 | tf_op jit(solution)/shard_map/partial_sums/pallas_call | solution.py:129
  84.1 3.0 %collective-permute-start = (bf16[272,256]{1,0:T(8,128)(2,1)}, bf16[272,256]{1,0:T(8,128)(2,1)S(1)}, u32[]{:S(2)}, u32[]{:S(2)}) collective-permute-start(bf16[272,256]{1,0:T(8,128)(2,1)} %get-tuple-element.7), channel_id=1, source_target_pairs={{0,16},{16,32},{32,48},{48,0},{1,17},{17,33},{33,49},{49,1},{2,18}... | collective-permute-start | bytes 417800 | tf_op jit(solution)/shard_map/ppermute | solution.py:251
  87.1 4.2 %collective-permute-start.1 = (bf16[272,256]{1,0:T(8,128)(2,1)}, bf16[272,256]{1,0:T(8,128)(2,1)S(1)}, u32[]{:S(2)}, u32[]{:S(2)}) collective-permute-start(bf16[272,256]{1,0:T(8,128)(2,1)} %get-tuple-element.8), channel_id=1, source_target_pairs={{0,32},{16,48},{32,0},{48,16},{1,33},{17,49},{33,1},{49,17},{2,34}... | collective-permute-start | bytes 417800 | tf_op jit(solution)/shard_map/ppermute | solution.py:251
  91.3 2.4 %collective-permute-start.2 = (bf16[272,256]{1,0:T(8,128)(2,1)}, bf16[272,256]{1,0:T(8,128)(2,1)S(1)}, u32[]{:S(2)}, u32[]{:S(2)}) collective-permute-start(bf16[272,256]{1,0:T(8,128)(2,1)} %get-tuple-element.9), channel_id=1, source_target_pairs={{0,48},{16,0},{32,16},{48,32},{1,49},{17,1},{33,17},{49,33},{2,50}... | collective-permute-start | bytes 417800 | tf_op jit(solution)/shard_map/ppermute | solution.py:251
  93.7 2.6 %collective-permute-done.refs_1_ = bf16[272,256]{1,0:T(8,128)(2,1)S(1)} collective-permute-done((bf16[272,256]{1,0:T(8,128)(2,1)}, bf16[272,256]{1,0:T(8,128)(2,1)S(1)}, u32[]{:S(2)}, u32[]{:S(2)}) %collective-permute-start) | collective-permute-done | bytes 139296 | tf_op jit(solution)/shard_map/ppermute | solution.py:251
  96.3 4.8 %collective-permute-done.1.refs_2_ = bf16[272,256]{1,0:T(8,128)(2,1)S(1)} collective-permute-done((bf16[272,256]{1,0:T(8,128)(2,1)}, bf16[272,256]{1,0:T(8,128)(2,1)S(1)}, u32[]{:S(2)}, u32[]{:S(2)}) %collective-permute-start.1) | collective-permute-done | bytes 139296 | tf_op jit(solution)/shard_map/ppermute | solution.py:251
  101.1 3.5 %collective-permute-done.2.refs_3_ = bf16[272,256]{1,0:T(8,128)(2,1)S(1)} collective-permute-done((bf16[272,256]{1,0:T(8,128)(2,1)}, bf16[272,256]{1,0:T(8,128)(2,1)S(1)}, u32[]{:S(2)}, u32[]{:S(2)}) %collective-permute-start.2) | collective-permute-done | bytes 139296 | tf_op jit(solution)/shard_map/ppermute | solution.py:251
  104.6 0.6 copy-done.4
  105.3 1.9 %average.1.refs_0_ = bf16[256,256]{1,0:T(8,128)(2,1)} custom-call(bf16[272,256]{1,0:T(8,128)(2,1)} %get-tuple-element.6.refs_0_, bf16[272,256]{1,0:T(8,128)(2,1)} %copy-done.2, bf16[272,256]{1,0:T(8,128)(2,1)} %copy-done.3, bf16[272,256]{1,0:T(8,128)(2,1)} %copy-done.4), custom_call_target="tpu_custom_call" | custom-call | flops 655360 | bytes 1179648 | tf_op jit(solution)/shard_map/average/pallas_call | solution.py:155
  107.2 3.3 %collective-permute-start.5 = (bf16[256,256]{1,0:T(8,128)(2,1)}, bf16[256,256]{1,0:T(8,128)(2,1)S(1)}, u32[]{:S(2)}, u32[]{:S(2)}) collective-permute-start(bf16[256,256]{1,0:T(8,128)(2,1)} %average.1.refs_0_), channel_id=1, source_target_pairs={{0,48},{16,0},{32,16},{48,32},{1,49},{17,1},{33,17},{49,33},{2,50}... | collective-permute-start | bytes 393224 | tf_op jit(solution)/shard_map/ppermute | solution.py:251
  110.5 1.4 collective-permute-start.4
  111.9 2.1 %collective-permute-start.3 = (bf16[256,256]{1,0:T(8,128)(2,1)}, bf16[256,256]{1,0:T(8,128)(2,1)S(1)}, u32[]{:S(2)}, u32[]{:S(2)}) collective-permute-start(bf16[256,256]{1,0:T(8,128)(2,1)} %average.1.refs_0_), channel_id=1, source_target_pairs={{0,16},{16,32},{32,48},{48,0},{1,17},{17,33},{33,49},{49,1},{2,18}... | collective-permute-start | bytes 393224 | tf_op jit(solution)/shard_map/ppermute | solution.py:251
  114.0 6.5 %collective-permute-done.5.refs_3_ = bf16[256,256]{1,0:T(8,128)(2,1)S(1)} collective-permute-done((bf16[256,256]{1,0:T(8,128)(2,1)}, bf16[256,256]{1,0:T(8,128)(2,1)S(1)}, u32[]{:S(2)}, u32[]{:S(2)}) %collective-permute-start.5) | collective-permute-done | bytes 131104 | tf_op jit(solution)/shard_map/ppermute | solution.py:251
  120.5 4.4 %collective-permute-done.4.refs_2_ = bf16[256,256]{1,0:T(8,128)(2,1)S(1)} collective-permute-done((bf16[256,256]{1,0:T(8,128)(2,1)}, bf16[256,256]{1,0:T(8,128)(2,1)S(1)}, u32[]{:S(2)}, u32[]{:S(2)}) %collective-permute-start.4) | collective-permute-done | bytes 131104 | tf_op jit(solution)/shard_map/ppermute | solution.py:251
  124.9 0.0 collective-permute-done.3.refs_1_
  124.9 0.6 copy-done.6
  125.5 0.7 copy-done.7
  126.2 5.6 %subtract.1 = bf16[64,80,256]{2,1,0:T(8,128)(2,1)} custom-call(s32[1]{0:T(128)} %bitcast.z_ref, f32[64,8,128]{2,1,0:T(8,128)} %copy-done.1, bf16[4096,256]{1,0:T(8,128)(2,1)} %bitcast.7, bf16[256,256]{1,0:T(8,128)(2,1)} %average.1.refs_0_, bf16[256,256]{1,0:T(8,128)(2,1)} %copy-done.7, bf16[256,256]{1,0:T(8,128)(2,1)} %copy-done.6, bf16[256,256]{1,0:T(8,128)(2,1)} %copy-done.5), custom_call_target="tpu_custom_call" | custom-call | flops 2147483648 | bytes 4718592 | tf_op jit(solution)/shard_map/subtract/pallas_call | solution.py:199
  131.8 40.6 %all_to_all.15.back_ref.coadd_ref = bf16[64,80,256]{2,1,0:T(8,128)(2,1)} all-to-all(bf16[64,80,256]{2,1,0:T(8,128)(2,1)} %subtract.1), channel_id=1, replica_groups=mesh['y'=4,'far'=4,'near'=2,'x'=4,'c'=2] {'y','near','x','c'}, dimensions={0} | all-to-all | bytes 5242880 | tf_op jit(solution)/shard_map/all_to_all | solution.py:275
  172.4 6.0 %place.1 = (bf16[64,128,128]{2,1,0:T(8,128)(2,1)}, bf16[16,16384]{1,0:T(8,128)(2,1)}) custom-call(bf16[64,80,256]{2,1,0:T(8,128)(2,1)} %all_to_all.15.back_ref.coadd_ref, bf16[64,80,256]{2,1,0:T(8,128)(2,1)} %all_to_all.15.back_ref.coadd_ref), custom_call_target="tpu_custom_call" | custom-call | bytes 4194304 | tf_op jit(solution)/shard_map/place/pallas_call | solution.py:228
  (14 shorter events, 0.0 us)
Async XLA Ops:
  2.9 35.2 %all-to-all-start = ((f32[64,8,128]{2,1,0:T(8,128)}), f32[64,8,128]{2,1,0:T(8,128)S(1)}, u32[]{:S(2)}, u32[]{:S(2)}) async-start(f32[64,8,128]{2,1,0:T(8,128)} %broadcast_in_dim.3), calls=%async_computation | async-start | bytes 524288 | tf_op jit(solution)/shard_map/all_to_all | solution.py:266
  38.1 0.7 copy-start.1
  38.8 37.9 %all-to-all-start.1 = ((bf16[64,64,256]{2,1,0:T(8,128)(2,1)}), bf16[64,64,256]{2,1,0:T(8,128)(2,1)S(1)}, u32[]{:S(2)}, u32[]{:S(2)}) async-start(bf16[64,64,256]{2,1,0:T(8,128)(2,1)} %convolve.1), calls=%async_computation.1 | async-start | bytes 4194304 | tf_op jit(solution)/shard_map/all_to_all | solution.py:269
  76.6 1.3 copy-start
  84.1 12.1 %collective-permute-start = (bf16[272,256]{1,0:T(8,128)(2,1)}, bf16[272,256]{1,0:T(8,128)(2,1)S(1)}, u32[]{:S(2)}, u32[]{:S(2)}) collective-permute-start(bf16[272,256]{1,0:T(8,128)(2,1)} %get-tuple-element.7), channel_id=1, source_target_pairs={{0,16},{16,32},{32,48},{48,0},{1,17},{17,33},{33,49},{49,1},{2,18}... | collective-permute-start | bytes 417800 | tf_op jit(solution)/shard_map/ppermute | solution.py:251
  87.1 14.0 %collective-permute-start.1 = (bf16[272,256]{1,0:T(8,128)(2,1)}, bf16[272,256]{1,0:T(8,128)(2,1)S(1)}, u32[]{:S(2)}, u32[]{:S(2)}) collective-permute-start(bf16[272,256]{1,0:T(8,128)(2,1)} %get-tuple-element.8), channel_id=1, source_target_pairs={{0,32},{16,48},{32,0},{48,16},{1,33},{17,49},{33,1},{49,17},{2,34}... | collective-permute-start | bytes 417800 | tf_op jit(solution)/shard_map/ppermute | solution.py:251
  91.3 13.3 %collective-permute-start.2 = (bf16[272,256]{1,0:T(8,128)(2,1)}, bf16[272,256]{1,0:T(8,128)(2,1)S(1)}, u32[]{:S(2)}, u32[]{:S(2)}) collective-permute-start(bf16[272,256]{1,0:T(8,128)(2,1)} %get-tuple-element.9), channel_id=1, source_target_pairs={{0,48},{16,0},{32,16},{48,32},{1,49},{17,1},{33,17},{49,33},{2,50}... | collective-permute-start | bytes 417800 | tf_op jit(solution)/shard_map/ppermute | solution.py:251
  96.3 8.3 %copy-start.2 = (bf16[272,256]{1,0:T(8,128)(2,1)}, bf16[272,256]{1,0:T(8,128)(2,1)S(1)}, u32[]{:S(2)}) copy-start(bf16[272,256]{1,0:T(8,128)(2,1)S(1)} %collective-permute-done.refs_1_) | copy-start | bytes 417796
  101.1 3.5 %copy-start.3 = (bf16[272,256]{1,0:T(8,128)(2,1)}, bf16[272,256]{1,0:T(8,128)(2,1)S(1)}, u32[]{:S(2)}) copy-start(bf16[272,256]{1,0:T(8,128)(2,1)S(1)} %collective-permute-done.1.refs_2_) | copy-start | bytes 417796
  104.6 0.7 copy-start.4
  107.2 13.4 %collective-permute-start.5 = (bf16[256,256]{1,0:T(8,128)(2,1)}, bf16[256,256]{1,0:T(8,128)(2,1)S(1)}, u32[]{:S(2)}, u32[]{:S(2)}) collective-permute-start(bf16[256,256]{1,0:T(8,128)(2,1)} %average.1.refs_0_), channel_id=1, source_target_pairs={{0,48},{16,0},{32,16},{48,32},{1,49},{17,1},{33,17},{49,33},{2,50}... | collective-permute-start | bytes 393224 | tf_op jit(solution)/shard_map/ppermute | solution.py:251
  110.5 14.4 %collective-permute-start.4 = (bf16[256,256]{1,0:T(8,128)(2,1)}, bf16[256,256]{1,0:T(8,128)(2,1)S(1)}, u32[]{:S(2)}, u32[]{:S(2)}) collective-permute-start(bf16[256,256]{1,0:T(8,128)(2,1)} %average.1.refs_0_), channel_id=1, source_target_pairs={{0,32},{16,48},{32,0},{48,16},{1,33},{17,49},{33,1},{49,17},{2,34}... | collective-permute-start | bytes 393224 | tf_op jit(solution)/shard_map/ppermute | solution.py:251
  111.9 13.0 %collective-permute-start.3 = (bf16[256,256]{1,0:T(8,128)(2,1)}, bf16[256,256]{1,0:T(8,128)(2,1)S(1)}, u32[]{:S(2)}, u32[]{:S(2)}) collective-permute-start(bf16[256,256]{1,0:T(8,128)(2,1)} %average.1.refs_0_), channel_id=1, source_target_pairs={{0,16},{16,32},{32,48},{48,0},{1,17},{17,33},{33,49},{49,1},{2,18}... | collective-permute-start | bytes 393224 | tf_op jit(solution)/shard_map/ppermute | solution.py:251
  120.5 4.4 %copy-start.5 = (bf16[256,256]{1,0:T(8,128)(2,1)}, bf16[256,256]{1,0:T(8,128)(2,1)S(1)}, u32[]{:S(2)}) copy-start(bf16[256,256]{1,0:T(8,128)(2,1)S(1)} %collective-permute-done.5.refs_3_) | copy-start | bytes 393220
  124.9 0.6 copy-start.6
  125.5 0.7 copy-start.7

commit v2 on v1

v2 whole, which is shorter than its diff:
```python
import functools

import jax
import jax.numpy as jnp
from jax import lax
from jax.experimental import pallas as pl
from jax.experimental.pallas import tpu as pltpu
from jax.sharding import Mesh, PartitionSpec as P

BLOCKS = 16
SIDE = 128
GROUP = 16
HEAD = 8
TAIL = 16
STRIDE = 132
FAR = "far"
PLANE = ("c", "x", "near", "y")
EVERY = ("y", "far", "near", "x", "c")
BF16 = jnp.bfloat16
F32 = jnp.float32


def params(limit=63 << 20):
    return pltpu.CompilerParams(vmem_limit_bytes=limit)


def cost(flops, nbytes):
    return pl.CostEstimate(flops=flops, bytes_accessed=nbytes, transcendentals=0)


def band(taps_ref, b, half):
    line = jnp.broadcast_to(taps_ref[b : b + 1, :], (SIDE, SIDE))
    moved = pltpu.roll(line, 0, 1, stride=1, stride_axis=0)
    rows = lax.broadcasted_iota(jnp.int32, (SIDE, SIDE), 0)
    columns = lax.broadcasted_iota(jnp.int32, (SIDE, SIDE), 1)
    return jnp.where(jnp.abs(columns - rows) <= half, moved, 0.0)


def conv_kernel(nb, half, coef_ref, x_ref, col_taps_ref, row_taps_ref, out_ref, col_ref, row_ref, taps_ref, z_ref, m_ref):
    step = pl.program_id(0)

    @pl.when(step == 0)
    def _():
        for source, target, flip in ((col_taps_ref, col_ref, True), (row_taps_ref, row_ref, False)):
            taps_ref[...] = jnp.zeros_like(taps_ref)
            taps_ref[:nb, : 2 * half + 1] = source[...].astype(F32)
            taps_ref[...] = pltpu.roll(taps_ref[...], SIDE - half, 1)
            for b in range(nb):
                matrix = band(taps_ref, b, half)
                matrix = matrix.T if flip else matrix
                target[:, b * SIDE : (b + 1) * SIDE] = matrix.astype(BF16)

    x = x_ref[...].reshape(GROUP * SIDE, SIDE)
    for first in range(0, nb, 2):
        some = min(2, nb - first)
        inner = jnp.dot(x, col_ref[:, first * SIDE : (first + some) * SIDE], preferred_element_type=F32)
        for k in range(some):
            b = first + k
            for p in range(GROUP):
                part = inner[p * SIDE : (p + 1) * SIDE, k * SIDE : (k + 1) * SIDE]
                z_ref[p // 2, b * SIDE : (b + 1) * SIDE, (p % 2) * SIDE : (p % 2 + 1) * SIDE] = (
                    part * coef_ref[step * GROUP + p, b]
                ).astype(BF16)
    for pair in range(GROUP // 2):
        outer = jnp.dot(row_ref[...], z_ref[pair], preferred_element_type=F32)
        for h in range(2):
            at = (2 * pair + h) * STRIDE
            m_ref[at : at + SIDE] = outer[:, h * SIDE : (h + 1) * SIDE]
    per = SIDE // out_ref.shape[0]
    for i in range(SIDE):
        t, k = divmod(i, per)
        out_ref[t, :, k * SIDE : (k + 1) * SIDE] = m_ref[pl.ds(i, GROUP, stride=STRIDE), :].astype(BF16)


def convolve(pieces, coeffs, col_taps, row_taps, chunks):
    count = pieces.shape[0]
    nb, width = row_taps.shape
    padded = -(-nb // 8) * 8
    return pl.pallas_call(
        functools.partial(conv_kernel, nb, (width - 1) // 2),
        grid=(count // GROUP,),
        in_specs=[
            pl.BlockSpec(memory_space=pltpu.SMEM),
            pl.BlockSpec((GROUP, SIDE, SIDE), lambda g: (g, 0, 0)),
            pl.BlockSpec((nb, width), lambda g: (0, 0)),
            pl.BlockSpec((nb, width), lambda g: (0, 0)),
        ],
        out_specs=pl.BlockSpec((chunks, GROUP, SIDE * SIDE // chunks), lambda g: (0, g, 0)),
        out_shape=jax.ShapeDtypeStruct((chunks, count, SIDE * SIDE // chunks), BF16),
        scratch_shapes=[
            pltpu.VMEM((SIDE, nb * SIDE), BF16),
            pltpu.VMEM((SIDE, nb * SIDE), BF16),
            pltpu.VMEM((padded, SIDE), F32),
            pltpu.VMEM((GROUP // 2, nb * SIDE, 2 * SIDE), BF16),
            pltpu.VMEM((GROUP * STRIDE, SIDE), F32),
        ],
        compiler_params=params(),
        cost_estimate=cost(count * nb * SIDE**3 * 4, count * SIDE * SIDE * 4),
        name="convolve",
    )(coeffs, pieces, col_taps, row_taps)


def describe_kernel(steps, own_rows, z_ref, info_ref, line_ref, out_ref):
    sources = info_ref.shape[0]
    left = lax.broadcasted_iota(jnp.int32, (1, SIDE), 1) < SIDE // 2
    for a in range(sources // 2):
        span = slice(a * SIDE, (a + 1) * SIDE)
        for line in range(2):
            even = info_ref[2 * a, line : line + 1, :]
            odd = pltpu.roll(info_ref[2 * a + 1, line : line + 1, :], SIDE // 2, 1)
            line_ref[line : line + 1, span] = jnp.where(left, even, odd)
    row, weight = line_ref[:1, :].astype(jnp.int32), line_ref[1:2, :]
    index = lax.broadcasted_iota(jnp.int32, (own_rows, row.shape[1]), 0)
    for k in range(steps):
        first = lax.rem(z_ref[0] + k, steps) * own_rows
        marks = jnp.where(index == row - first, weight, 0.0)
        total = jnp.broadcast_to(jnp.sum(marks, axis=1, keepdims=True), (own_rows, SIDE))
        total = total.T[:TAIL]
        high = total.astype(BF16).astype(F32)
        middle = (total - high).astype(BF16).astype(F32)
        low = total - high - middle
        line = lax.broadcasted_iota(jnp.int32, total.shape, 0)
        terms = jnp.where(line == 0, high, jnp.where(line == 1, middle, jnp.where(line == 2, low, 0.0)))
        out_ref[k * TAIL : (k + 1) * TAIL, :] = terms.astype(BF16)


def describe(z, info, steps, own_rows):
    held = info.shape[0] * SIDE // 2
    vmem = pl.BlockSpec(memory_space=pltpu.VMEM)
    return pl.pallas_call(
        functools.partial(describe_kernel, steps, own_rows),
        in_specs=[pl.BlockSpec(memory_space=pltpu.SMEM), vmem],
        out_specs=[vmem] * 2,
        out_shape=[jax.ShapeDtypeStruct((HEAD, held), F32)]
        + [jax.ShapeDtypeStruct((steps * TAIL, own_rows), BF16)],
        compiler_params=params(),
        cost_estimate=cost(4 * held * steps * own_rows, held * SIDE * 4),
        name="describe",
    )(z, info)


def partial_kernel(steps, z_ref, line_ref, got_ref, terms_ref, *refs):
    outs, total_ref = refs[:steps], refs[steps]
    step = pl.program_id(0)
    total_rows = total_ref.shape[0]
    own_rows = total_rows // steps
    row, weight = line_ref[:1, :].astype(jnp.int32), line_ref[1:2, :]
    place = jnp.bitwise_and(row - z_ref[0] * own_rows, total_rows - 1)
    index = lax.broadcasted_iota(jnp.int32, (total_rows, row.shape[1]), 0)
    marks = jnp.where(index == place, weight, 0.0).astype(BF16)
    part = jnp.dot(marks, got_ref[...], preferred_element_type=F32)

    @pl.when(step == 0)
    def _():
        total_ref[...] = part

    @pl.when(step > 0)
    def _():
        total_ref[...] += part

    @pl.when(step == pl.num_programs(0) - 1)
    def _():
        for k in range(steps):
            outs[k][:own_rows, :] = total_ref[k * own_rows : (k + 1) * own_rows, :].astype(BF16)
            outs[k][own_rows:, :] = terms_ref[k * TAIL : (k + 1) * TAIL, :]


def partial_sums(z, lines, got, terms, steps, own_rows):
    held, width = got.shape
    some = held // 4
    return pl.pallas_call(
        functools.partial(partial_kernel, steps),
        grid=(held // some,),
        in_specs=[
            pl.BlockSpec(memory_space=pltpu.SMEM),
            pl.BlockSpec((HEAD, some), lambda g: (0, g)),
            pl.BlockSpec((some, width), lambda g: (g, 0)),
            pl.BlockSpec(terms.shape, lambda g: (0, 0)),
        ],
        out_specs=[pl.BlockSpec((own_rows + TAIL, width), lambda g: (0, 0))] * steps,
        out_shape=[jax.ShapeDtypeStruct((own_rows + TAIL, width), BF16)] * steps,
        scratch_shapes=[pltpu.VMEM((steps * own_rows, width), F32)],
        compiler_params=params(),
        cost_estimate=cost(2 * steps * own_rows * held * width, (held + steps * own_rows) * width * 2),
        name="partial_sums",
    )(z, lines, got, terms)


def average_kernel(own_rows, *refs):
    parts, out_ref = refs[:-1], refs[-1]
    terms = sum(ref[own_rows:, :].astype(F32) for ref in parts)
    line = jnp.sum(terms, axis=0, keepdims=True)
    below = jnp.maximum(jnp.broadcast_to(line, (SIDE, own_rows)).T, 1.0)
    total = sum(ref[:own_rows, :].astype(F32) for ref in parts)
    for k in range(total.shape[1] // SIDE):
        span = slice(k * SIDE, (k + 1) * SIDE)
        out_ref[:, span] = (total[:, span] / below).astype(BF16)


def average(parts, own_rows):
    width = parts[0].shape[1]
    vmem = pl.BlockSpec(memory_space=pltpu.VMEM)
    return pl.pallas_call(
        functools.partial(average_kernel, own_rows),
        in_specs=[vmem] * len(parts),
        out_specs=vmem,
        out_shape=jax.ShapeDtypeStruct((own_rows, width), BF16),
        compiler_params=params(),
        cost_estimate=cost(10 * own_rows * width, 18 * own_rows * width),
        name="average",
    )(*parts)


def subtract_kernel(count, sizes, line_ref, got_ref, coadd_ref, own_ref, out_ref):
    total_rows = coadd_ref.shape[0]
    sources = out_ref.shape[0]
    index = lax.broadcasted_iota(jnp.int32, (SIDE, total_rows), 1).astype(F32)
    marks = []
    for a in range(0, line_ref.shape[1], SIDE):
        column = jnp.broadcast_to(line_ref[:1, a : a + SIDE], (SIDE, SIDE)).T
        column = jnp.concatenate([column] * (total_rows // SIDE), axis=1)
        marks.append(jnp.where(index == column, 1.0, 0.0).astype(BF16))
    under = jnp.dot(jnp.concatenate(marks), coadd_ref[...], preferred_element_type=F32)
    diff = (got_ref[...].astype(F32) - under).astype(BF16)
    n_core, n_x, n_near, n_y = sizes
    for s in range(sources):
        out_ref[s, :count, :] = diff[s * count : (s + 1) * count]
        place = pl.program_id(0) * sources + s
        near = lax.rem(place // n_y, n_near)
        x = lax.rem(place // (n_y * n_near), n_x)
        core = place // (n_y * n_near * n_x)
        first = pl.multiple_of(((near * n_x + x) * n_core + core) * BLOCKS, BLOCKS)
        out_ref[s, count:, :] = own_ref[pl.ds(first, BLOCKS), :]


def subtract(lines, got, coadd, own, count, sizes):
    held, width = got.shape
    sources = held // count
    some = 16
    return pl.pallas_call(
        functools.partial(subtract_kernel, count, sizes),
        grid=(sources // some,),
        in_specs=[
            pl.BlockSpec((HEAD, some * count), lambda g: (0, g)),
            pl.BlockSpec((some * count, width), lambda g: (g, 0)),
            pl.BlockSpec(coadd.shape, lambda g: (0, 0)),
            pl.BlockSpec(own.shape, lambda g: (0, 0)),
        ],
        out_specs=pl.BlockSpec((some, count + BLOCKS, width), lambda g: (g, 0, 0)),
        out_shape=jax.ShapeDtypeStruct((sources, count + BLOCKS, width), BF16),
        compiler_params=params(),
        cost_estimate=cost(2 * coadd.shape[0] * held * width, (2 * held + coadd.shape[0]) * width * 2),
        name="subtract",
    )(lines, got, coadd, own)


def place_kernel(back_ref, coadd_ref, diff_ref, template_ref, m_ref):
    chunks, _, width = back_ref.shape
    per = width // SIDE
    for i in range(SIDE):
        t, k = divmod(i, per)
        m_ref[pl.ds(i, GROUP, stride=STRIDE), :] = back_ref[t, :, k * SIDE : (k + 1) * SIDE].astype(F32)
    for p in range(GROUP):
        diff_ref[p] = m_ref[p * STRIDE : p * STRIDE + SIDE, :].astype(BF16)
    for t in range(coadd_ref.shape[0]):
        template_ref[:, t * width : (t + 1) * width] = coadd_ref[t]


def place(back, count):
    chunks, _, width = back.shape
    steps = count // GROUP
    some = chunks // steps
    return pl.pallas_call(
        place_kernel,
        grid=(steps,),
        in_specs=[
            pl.BlockSpec((chunks, GROUP, width), lambda g: (0, g, 0)),
            pl.BlockSpec((some, BLOCKS, width), lambda g: (g, count // BLOCKS, 0)),
        ],
        out_specs=(
            pl.BlockSpec((GROUP, SIDE, SIDE), lambda g: (g, 0, 0)),
            pl.BlockSpec((BLOCKS, some * width), lambda g: (0, g)),
        ),
        out_shape=(
            jax.ShapeDtypeStruct((count, SIDE, SIDE), BF16),
            jax.ShapeDtypeStruct((BLOCKS, SIDE * SIDE), BF16),
        ),
        scratch_shapes=[pltpu.VMEM((GROUP * STRIDE, SIDE), F32)],
        compiler_params=params(),
        cost_estimate=cost(0, 4 * count * SIDE * SIDE),
        name="place",
    )(back, back)


def shift(array, by, steps):
    return lax.ppermute(array, FAR, [(i, (i + by) % steps) for i in range(steps)])


def body(pieces, row_taps, col_taps, coeffs, weights, blocks, routes):
    count = pieces.shape[0]
    steps = lax.axis_size(FAR)
    chunks = lax.axis_size(PLANE)
    own_rows = chunks // lax.axis_size("y") * BLOCKS
    sizes = tuple(lax.axis_size(name) for name in PLANE)
    z = lax.axis_index(FAR).astype(jnp.int32).reshape(1)
    others = sorted(range(1, steps), key=lambda k: -min(k, steps - k))

    row = jnp.pad((routes[:, 0] * BLOCKS + blocks).astype(F32), (0, SIDE - count))
    weight = jnp.pad(weights.astype(F32), (0, SIDE - count))
    line = lax.broadcasted_iota(jnp.int32, (chunks, HEAD, SIDE), 1)
    info = jnp.where(line == 0, row, weight)
    info = lax.all_to_all(info, PLANE, split_axis=0, concat_axis=0, tiled=True)

    sent = convolve(pieces, coeffs, col_taps, row_taps, chunks)
    got = lax.all_to_all(sent, PLANE, split_axis=0, concat_axis=0, tiled=True)
    got = got.reshape(chunks * count, -1)

    lines, terms = describe(z, info, steps, own_rows)
    sums = partial_sums(z, lines, got, terms, steps, own_rows)
    own = average([sums[0]] + [shift(sums[k], k, steps) for k in others], own_rows)
    coadd = lax.all_gather(own, FAR, axis=0, tiled=True)
    back = subtract(lines, got, coadd, own, count, sizes)
    back = lax.all_to_all(back, PLANE, split_axis=0, concat_axis=0, tiled=True)
    return place(back, count)


def solution(mesh):
    finer = Mesh(mesh.devices.reshape(4, 4, 2, 4, 2), EVERY)
    in_specs = (
        P(EVERY, None, None),
        P(),
        P(),
        P(EVERY, None),
        P(EVERY),
        P(EVERY),
        P(EVERY, None),
    )
    out_specs = (P(EVERY, None, None), P(EVERY[1:], None))
    return jax.shard_map(body, mesh=finer, in_specs=in_specs, out_specs=out_specs, check_vma=False)
```

time: 179 us -> 172 us (0.961)
  blocking collectives: 40.6 us -> 58.6 us
  waiting for transfers between devices: 50.8 us -> 34.6 us
  starting transfers between devices: 35.6 us -> 28.9 us
  local copies, waits for them, and re-layouts: 6.94 us -> 2.77 us
    all_gather x0 -> x1, blocking collectives: none -> 17.4 us  [body(): coadd = lax.all_gather(own, FAR, axis=0, tiled=True)]
    ppermute x6 -> x3, waiting for transfers between devices: 21.8 us -> 10.7 us  [shift(): lax.ppermute(array, FAR, [(i, (i + by) % steps) for i in range(steps)])]
    ppermute x6 -> x3, starting transfers between devices: 16.4 us -> 9.59 us  [shift(): lax.ppermute(array, FAR, [(i, (i + by) % steps) for i in range(steps)])]
    all_to_all x1, waiting for transfers between devices: 29 us -> 23.8 us  [body(): got = lax.all_to_all(sent, PLANE, split_axis=0, concat_axis=0, tiled=True)]
    pallas_call x2 -> x3, Pallas kernels: 11.8 us -> 15.7 us  [the longest x1 6.22 us: subtract(): pl.pallas_call(functools.partial(subtract_kernel, count, sizes), grid=(so...]
    unnamed x17 -> x9, local copies, waits for them, and re-layouts: 5.38 us -> 2.77 us
    pallas_call x1, Pallas kernels: 23.4 us -> 21.4 us  [convolve(): pl.pallas_call(functools.partial(conv_kernel, nb, (width - 1) // 2), grid...]
    pallas_call x1, Pallas kernels: 6.01 us -> 4.09 us  [place(): pl.pallas_call(place_kernel, grid=(steps,), in_specs=[pl.BlockSpec((chunk...]
  transfers between devices with their start and end apart: 8 -> 5, of which waited for: 6 -> 4; matrix products, arithmetic and copies ran while one was open for 1% -> 1% of each run, Pallas kernels for 13% -> 15%
where the time goes in v2:
time: 172 us; the launch traced here: 171 us
  blocking collectives  58.6 us (34%)
  Pallas kernels  43.1 us (25%)
  waiting for transfers between devices  34.6 us (20%)
  starting transfers between devices  28.9 us (17%)
  local copies, waits for them, and re-layouts  2.77 us (2%)
  other arithmetic  2.13 us (1%)
    all_to_all x1, blocking collectives, body(): back = lax.all_to_all(back, PLANE, split_axis=0, concat_axis=0, tiled=True)  41.2 us
    all_to_all x1, waiting for transfers between devices, body(): got = lax.all_to_all(sent, PLANE, split_axis=0, concat_axis=0, tiled=True)  23.8 us
    pallas_call x1, Pallas kernels, convolve(): pl.pallas_call(functools.partial(conv_kernel, nb, (width - 1) // 2), grid...  21.4 us
    all_gather x1, blocking collectives, body(): coadd = lax.all_gather(own, FAR, axis=0, tiled=True)  17.4 us
    ppermute x3, waiting for transfers between devices, shift(): lax.ppermute(array, FAR, [(i, (i + by) % steps) for i in range(steps)])  10.7 us
    all_to_all x1, starting transfers between devices, body(): info = lax.all_to_all(info, PLANE, split_axis=0, concat_axis=0, tiled=True)  10.4 us
    ppermute x3, starting transfers between devices, shift(): lax.ppermute(array, FAR, [(i, (i + by) % steps) for i in range(steps)])  9.59 us
    all_to_all x1, starting transfers between devices, body(): got = lax.all_to_all(sent, PLANE, split_axis=0, concat_axis=0, tiled=True)  8.88 us
  transfers between devices with their start and end apart: 5, of which 4 were waited for; matrix products, arithmetic and copies ran while one was open for 1% of the time, Pallas kernels for 15%

profile of v2, /device:TPU:1, one launch (start us, length us, event | category | flops | bytes accessed | tf_op | source)
XLA Modules:
  0.0 170.8 jit_solution(14381909486861535962)
XLA Ops:
  0.6 0.7 pad_convert_fusion
  1.3 0.7 fusion
  2.0 0.8 broadcast_select_fusion
  2.8 10.4 %all-to-all-start = ((f32[64,8,128]{2,1,0:T(8,128)}), f32[64,8,128]{2,1,0:T(8,128)S(1)}, u32[]{:S(2)}, u32[]{:S(2)}) async-start(f32[64,8,128]{2,1,0:T(8,128)} %broadcast_select_fusion), calls=%async_computation | async-start | bytes 524288 | tf_op jit(solution)/shard_map/all_to_all | solution.py:312
  13.2 1.4 copy.9.coef_ref
  14.6 21.4 %convolve.1 = bf16[64,64,256]{2,1,0:T(8,128)(2,1)} custom-call(f32[64,21]{1,0:T(8,128)} %copy.9.coef_ref, bf16[64,128,128]{2,1,0:T(8,128)(2,1)} %x_ref.1, bf16[21,41]{1,0:T(8,128)(2,1)} %col_taps_ref.1, bf16[21,41]{1,0:T(8,128)(2,1)} %row_taps_ref.1), custom_call_target="tpu_custom_call" | custom-call | flops 11274289152 | bytes 4194304 | tf_op jit(solution)/shard_map/convolve/pallas_call | solution.py:79
  36.1 0.0 all-to-all-done.info_ref
  36.1 0.0 copy-start
  36.1 0.7 copy-done
  36.8 8.9 %all-to-all-start.1 = ((bf16[64,64,256]{2,1,0:T(8,128)(2,1)}), bf16[64,64,256]{2,1,0:T(8,128)(2,1)}, u32[]{:S(2)}, u32[]{:S(2)}) async-start(bf16[64,64,256]{2,1,0:T(8,128)(2,1)} %convolve.1), calls=%async_computation.1 | async-start | bytes 4194304 | tf_op jit(solution)/shard_map/all_to_all | solution.py:315
  45.7 4.1 %describe.1 = (f32[8,4096]{1,0:T(8,128)}, bf16[64,256]{1,0:T(8,128)(2,1)}) custom-call(s32[1]{0:T(128)} %bitcast.z_ref, f32[64,8,128]{2,1,0:T(8,128)} %copy-done), custom_call_target="tpu_custom_call" | custom-call | flops 16777216 | bytes 2097152 | tf_op jit(solution)/shard_map/describe/pallas_call | solution.py:130
  49.7 23.8 %all-to-all-done.1 = bf16[64,64,256]{2,1,0:T(8,128)(2,1)} async-done(((bf16[64,64,256]{2,1,0:T(8,128)(2,1)}), bf16[64,64,256]{2,1,0:T(8,128)(2,1)}, u32[]{:S(2)}, u32[]{:S(2)}) %all-to-all-start.1) | async-done | bytes 2097184 | tf_op jit(solution)/shard_map/all_to_all | solution.py:315
  73.6 5.4 %partial_sums.1 = (bf16[272,256]{1,0:T(8,128)(2,1)}, bf16[272,256]{1,0:T(8,128)(2,1)}, bf16[272,256]{1,0:T(8,128)(2,1)}, bf16[272,256]{1,0:T(8,128)(2,1)}) custom-call(s32[1]{0:T(128)} %bitcast.z_ref, f32[8,4096]{1,0:T(8,128)} %get-tuple-element.8.line_ref, bf16[4096,256]{1,0:T(8,128)(2,1)} %bitcast.2.got_ref, bf16[64,256]{1,0:T(8,128)(2,1)} %get-tuple-element.9.terms_ref), custom_call_target="tpu_custom_call" | custom-call | flops 2147483648 | bytes 2621440 | tf_op jit(solution)/shard_map/partial_sums/pallas_call | solution.py:171
  79.0 6.0 %collective-permute-start = (bf16[272,256]{1,0:T(8,128)(2,1)}, bf16[272,256]{1,0:T(8,128)(2,1)S(1)}, u32[]{:S(2)}, u32[]{:S(2)}) collective-permute-start(bf16[272,256]{1,0:T(8,128)(2,1)} %get-tuple-element.11), channel_id=1, source_target_pairs={{0,32},{16,48},{32,0},{48,16},{1,33},{17,49},{33,1},{49,17},{2,34}... | collective-permute-start | bytes 417800 | tf_op jit(solution)/shard_map/ppermute | solution.py:296
  85.0 1.2 collective-permute-start.1
  86.2 2.4 %collective-permute-start.2 = (bf16[272,256]{1,0:T(8,128)(2,1)}, bf16[272,256]{1,0:T(8,128)(2,1)S(1)}, u32[]{:S(2)}, u32[]{:S(2)}) collective-permute-start(bf16[272,256]{1,0:T(8,128)(2,1)} %get-tuple-element.13), channel_id=1, source_target_pairs={{0,48},{16,0},{32,16},{48,32},{1,49},{17,1},{33,17},{49,33},{2,50}... | collective-permute-start | bytes 417800 | tf_op jit(solution)/shard_map/ppermute | solution.py:296
  88.6 0.4 collective-permute-done.refs_1_
  89.1 0.0 copy-start.1
  89.1 7.9 %collective-permute-done.1.refs_2_ = bf16[272,256]{1,0:T(8,128)(2,1)S(1)} collective-permute-done((bf16[272,256]{1,0:T(8,128)(2,1)}, bf16[272,256]{1,0:T(8,128)(2,1)S(1)}, u32[]{:S(2)}, u32[]{:S(2)}) %collective-permute-start.1) | collective-permute-done | bytes 139296 | tf_op jit(solution)/shard_map/ppermute | solution.py:296
  96.9 0.0 copy-start.2
  96.9 2.4 %collective-permute-done.2.refs_3_ = bf16[272,256]{1,0:T(8,128)(2,1)S(1)} collective-permute-done((bf16[272,256]{1,0:T(8,128)(2,1)}, bf16[272,256]{1,0:T(8,128)(2,1)S(1)}, u32[]{:S(2)}, u32[]{:S(2)}) %collective-permute-start.2) | collective-permute-done | bytes 139296 | tf_op jit(solution)/shard_map/ppermute | solution.py:296
  99.3 0.0 copy-start.3
  99.3 0.0 copy-done.1
  99.3 0.0 copy-done.2
  99.3 0.7 copy-done.3
  100.0 1.9 %average.1.own_ref = bf16[256,256]{1,0:T(8,128)(2,1)} custom-call(bf16[272,256]{1,0:T(8,128)(2,1)} %get-tuple-element.10.refs_0_, bf16[272,256]{1,0:T(8,128)(2,1)} %copy-done.1, bf16[272,256]{1,0:T(8,128)(2,1)} %copy-done.2, bf16[272,256]{1,0:T(8,128)(2,1)} %copy-done.3), custom_call_target="tpu_custom_call" | custom-call | flops 655360 | bytes 1179648 | tf_op jit(solution)/shard_map/average/pallas_call | solution.py:203
  101.9 17.4 %all_gather.3.coadd_ref = bf16[1024,256]{1,0:T(8,128)(2,1)} all-gather(bf16[256,256]{1,0:T(8,128)(2,1)} %average.1.own_ref), channel_id=1, replica_groups=mesh['y'=4,'far'=4,'near'=2,'x'=4,'c'=2] {'far'}, dimensions={0}, use_global_device_ids=true | all-gather | bytes 655360 | tf_op jit(solution)/shard_map/all_gather | solution.py:321
  119.3 6.2 %subtract.1 = bf16[64,80,256]{2,1,0:T(8,128)(2,1)} custom-call(f32[8,4096]{1,0:T(8,128)} %get-tuple-element.8.line_ref, bf16[4096,256]{1,0:T(8,128)(2,1)} %bitcast.2.got_ref, bf16[1024,256]{1,0:T(8,128)(2,1)} %all_gather.3.coadd_ref, bf16[256,256]{1,0:T(8,128)(2,1)} %average.1.own_ref), custom_call_target="tpu_custom_call" | custom-call | flops 2147483648 | bytes 4718592 | tf_op jit(solution)/shard_map/subtract/pallas_call | solution.py:240
  125.5 41.2 %all_to_all.15.back_ref.coadd_ref = bf16[64,80,256]{2,1,0:T(8,128)(2,1)} all-to-all(bf16[64,80,256]{2,1,0:T(8,128)(2,1)} %subtract.1), channel_id=1, replica_groups=mesh['y'=4,'far'=4,'near'=2,'x'=4,'c'=2] {'c','x','near','y'}, dimensions={0} | all-to-all | bytes 5242880 | tf_op jit(solution)/shard_map/all_to_all | solution.py:323
  166.7 4.1 %place.1 = (bf16[64,128,128]{2,1,0:T(8,128)(2,1)}, bf16[16,16384]{1,0:T(8,128)(2,1)}) custom-call(bf16[64,80,256]{2,1,0:T(8,128)(2,1)} %all_to_all.15.back_ref.coadd_ref, bf16[64,80,256]{2,1,0:T(8,128)(2,1)} %all_to_all.15.back_ref.coadd_ref), custom_call_target="tpu_custom_call" | custom-call | bytes 4194304 | tf_op jit(solution)/shard_map/place/pallas_call | solution.py:273
  (2 shorter events, 0.0 us)
Async XLA Ops:
  2.8 33.3 %all-to-all-start = ((f32[64,8,128]{2,1,0:T(8,128)}), f32[64,8,128]{2,1,0:T(8,128)S(1)}, u32[]{:S(2)}, u32[]{:S(2)}) async-start(f32[64,8,128]{2,1,0:T(8,128)} %broadcast_select_fusion), calls=%async_computation | async-start | bytes 524288 | tf_op jit(solution)/shard_map/all_to_all | solution.py:312
  36.1 0.7 copy-start
  36.8 36.8 %all-to-all-start.1 = ((bf16[64,64,256]{2,1,0:T(8,128)(2,1)}), bf16[64,64,256]{2,1,0:T(8,128)(2,1)}, u32[]{:S(2)}, u32[]{:S(2)}) async-start(bf16[64,64,256]{2,1,0:T(8,128)(2,1)} %convolve.1), calls=%async_computation.1 | async-start | bytes 4194304 | tf_op jit(solution)/shard_map/all_to_all | solution.py:315
  79.0 10.0 %collective-permute-start = (bf16[272,256]{1,0:T(8,128)(2,1)}, bf16[272,256]{1,0:T(8,128)(2,1)S(1)}, u32[]{:S(2)}, u32[]{:S(2)}) collective-permute-start(bf16[272,256]{1,0:T(8,128)(2,1)} %get-tuple-element.11), channel_id=1, source_target_pairs={{0,32},{16,48},{32,0},{48,16},{1,33},{17,49},{33,1},{49,17},{2,34}... | collective-permute-start | bytes 417800 | tf_op jit(solution)/shard_map/ppermute | solution.py:296
  85.0 11.9 %collective-permute-start.1 = (bf16[272,256]{1,0:T(8,128)(2,1)}, bf16[272,256]{1,0:T(8,128)(2,1)S(1)}, u32[]{:S(2)}, u32[]{:S(2)}) collective-permute-start(bf16[272,256]{1,0:T(8,128)(2,1)} %get-tuple-element.12), channel_id=1, source_target_pairs={{0,16},{16,32},{32,48},{48,0},{1,17},{17,33},{33,49},{49,1},{2,18}... | collective-permute-start | bytes 417800 | tf_op jit(solution)/shard_map/ppermute | solution.py:296
  86.2 13.1 %collective-permute-start.2 = (bf16[272,256]{1,0:T(8,128)(2,1)}, bf16[272,256]{1,0:T(8,128)(2,1)S(1)}, u32[]{:S(2)}, u32[]{:S(2)}) collective-permute-start(bf16[272,256]{1,0:T(8,128)(2,1)} %get-tuple-element.13), channel_id=1, source_target_pairs={{0,48},{16,0},{32,16},{48,32},{1,49},{17,1},{33,17},{49,33},{2,50}... | collective-permute-start | bytes 417800 | tf_op jit(solution)/shard_map/ppermute | solution.py:296
  89.1 10.3 %copy-start.1 = (bf16[272,256]{1,0:T(8,128)(2,1)}, bf16[272,256]{1,0:T(8,128)(2,1)S(1)}, u32[]{:S(2)}) copy-start(bf16[272,256]{1,0:T(8,128)(2,1)S(1)} %collective-permute-done.refs_1_) | copy-start | bytes 417796
  96.9 2.4 %copy-start.2 = (bf16[272,256]{1,0:T(8,128)(2,1)}, bf16[272,256]{1,0:T(8,128)(2,1)S(1)}, u32[]{:S(2)}) copy-start(bf16[272,256]{1,0:T(8,128)(2,1)S(1)} %collective-permute-done.1.refs_2_) | copy-start | bytes 417796
  99.3 0.7 copy-start.3

commit v3 on v2

--- a/solution.py
+++ b/solution.py
@@ -139,47 +139,26 @@
     )(z, info)
 
 
-def partial_kernel(steps, z_ref, line_ref, got_ref, terms_ref, *refs):
-    outs, total_ref = refs[:steps], refs[steps]
-    step = pl.program_id(0)
-    total_rows = total_ref.shape[0]
-    own_rows = total_rows // steps
+def partial_kernel(steps, z_ref, line_ref, got_ref, terms_ref, *outs):
+    own_rows = outs[0].shape[0] - TAIL
     row, weight = line_ref[:1, :].astype(jnp.int32), line_ref[1:2, :]
-    place = jnp.bitwise_and(row - z_ref[0] * own_rows, total_rows - 1)
-    index = lax.broadcasted_iota(jnp.int32, (total_rows, row.shape[1]), 0)
-    marks = jnp.where(index == place, weight, 0.0).astype(BF16)
-    part = jnp.dot(marks, got_ref[...], preferred_element_type=F32)
-
-    @pl.when(step == 0)
-    def _():
-        total_ref[...] = part
-
-    @pl.when(step > 0)
-    def _():
-        total_ref[...] += part
-
-    @pl.when(step == pl.num_programs(0) - 1)
-    def _():
-        for k in range(steps):
-            outs[k][:own_rows, :] = total_ref[k * own_rows : (k + 1) * own_rows, :].astype(BF16)
-            outs[k][own_rows:, :] = terms_ref[k * TAIL : (k + 1) * TAIL, :]
+    place = jnp.bitwise_and(row - z_ref[0] * own_rows, steps * own_rows - 1)
+    index = lax.broadcasted_iota(jnp.int32, (own_rows, row.shape[1]), 0)
+    for k in range(steps):
+        marks = jnp.where(index + k * own_rows == place, weight, 0.0).astype(BF16)
+        part = jnp.dot(marks, got_ref[...], preferred_element_type=F32)
+        outs[k][:own_rows, :] = part.astype(BF16)
+        outs[k][own_rows:, :] = terms_ref[k * TAIL : (k + 1) * TAIL, :]
 
 
 def partial_sums(z, lines, got, terms, steps, own_rows):
     held, width = got.shape
-    some = held // 4
+    vmem = pl.BlockSpec(memory_space=pltpu.VMEM)
     return pl.pallas_call(
         functools.partial(partial_kernel, steps),
-        grid=(held // some,),
-        in_specs=[
-            pl.BlockSpec(memory_space=pltpu.SMEM),
-            pl.BlockSpec((HEAD, some), lambda g: (0, g)),
-            pl.BlockSpec((some, width), lambda g: (g, 0)),
-            pl.BlockSpec(terms.shape, lambda g: (0, 0)),
-        ],
-        out_specs=[pl.BlockSpec((own_rows + TAIL, width), lambda g: (0, 0))] * steps,
+        in_specs=[pl.BlockSpec(memory_space=pltpu.SMEM)] + [vmem] * 3,
+        out_specs=[vmem] * steps,
         out_shape=[jax.ShapeDtypeStruct((own_rows + TAIL, width), BF16)] * steps,
-        scratch_shapes=[pltpu.VMEM((steps * own_rows, width), F32)],
         compiler_params=params(),
         cost_estimate=cost(2 * steps * own_rows * held * width, (held + steps * own_rows) * width * 2),
         name="partial_sums",
@@ -236,7 +215,7 @@
 def subtract(lines, got, coadd, own, count, sizes):
     held, width = got.shape
     sources = held // count
-    some = 16
+    some = 32
     return pl.pallas_call(
         functools.partial(subtract_kernel, count, sizes),
         grid=(sources // some,),
@@ -254,42 +233,62 @@
     )(lines, got, coadd, own)
 
 
-def place_kernel(back_ref, coadd_ref, diff_ref, template_ref, m_ref):
+def place_kernel(back_ref, diff_ref, template_ref, here_ref, rows_ref, done_ref, flat_ref, m_ref, in_sems, out_sems):
     chunks, _, width = back_ref.shape
     per = width // SIDE
-    for i in range(SIDE):
-        t, k = divmod(i, per)
-        m_ref[pl.ds(i, GROUP, stride=STRIDE), :] = back_ref[t, :, k * SIDE : (k + 1) * SIDE].astype(F32)
-    for p in range(GROUP):
-        diff_ref[p] = m_ref[p * STRIDE : p * STRIDE + SIDE, :].astype(BF16)
-    for t in range(coadd_ref.shape[0]):
-        template_ref[:, t * width : (t + 1) * width] = coadd_ref[t]
+    steps = here_ref.shape[0]
+    ins = [
+        pltpu.make_async_copy(back_ref.at[:, pl.ds(g * GROUP, GROUP)], here_ref.at[g], in_sems.at[g]) for g in range(steps)
+    ]
+    ins.append(pltpu.make_async_copy(back_ref.at[:, pl.ds(steps * GROUP, BLOCKS)], rows_ref, in_sems.at[steps]))
+    outs = [
+        pltpu.make_async_copy(done_ref.at[pl.ds(g * GROUP, GROUP)], diff_ref.at[pl.ds(g * GROUP, GROUP)], out_sems.at[g])
+        for g in range(steps)
+    ]
+    outs.append(pltpu.make_async_copy(flat_ref, template_ref, out_sems.at[steps]))
+    for copy in ins:
+        copy.start()
+    for g in range(steps):
+        ins[g].wait()
+        for i in range(SIDE):
+            t, k = divmod(i, per)
+            m_ref[g % 2, pl.ds(i, GROUP, stride=STRIDE), :] = here_ref[g, t, :, k * SIDE : (k + 1) * SIDE].astype(F32)
+        for p in range(GROUP):
+            done_ref[g * GROUP + p] = m_ref[g % 2, p * STRIDE : p * STRIDE + SIDE, :].astype(BF16)
+        outs[g].start()
+    ins[steps].wait()
+    for t in range(chunks):
+        flat_ref[:, t * width : (t + 1) * width] = rows_ref[t]
+    outs[steps].start()
+    for copy in outs:
+        copy.wait()
 
 
 def place(back, count):
     chunks, _, width = back.shape
     steps = count // GROUP
-    some = chunks // steps
+    any_space = pl.BlockSpec(memory_space=pl.ANY)
     return pl.pallas_call(
         place_kernel,
-        grid=(steps,),
-        in_specs=[
-            pl.BlockSpec((chunks, GROUP, width), lambda g: (0, g, 0)),
-            pl.BlockSpec((some, BLOCKS, width), lambda g: (g, count // BLOCKS, 0)),
-        ],
-        out_specs=(
-            pl.BlockSpec((GROUP, SIDE, SIDE), lambda g: (g, 0, 0)),
-            pl.BlockSpec((BLOCKS, some * width), lambda g: (0, g)),
-        ),
-        out_shape=(
+        in_specs=[any_space],
+        out_specs=[any_space, any_space],
+        out_shape=[
             jax.ShapeDtypeStruct((count, SIDE, SIDE), BF16),
             jax.ShapeDtypeStruct((BLOCKS, SIDE * SIDE), BF16),
-        ),
-        scratch_shapes=[pltpu.VMEM((GROUP * STRIDE, SIDE), F32)],
+        ],
+        scratch_shapes=[
+            pltpu.VMEM((steps, chunks, GROUP, width), BF16),
+            pltpu.VMEM((chunks, BLOCKS, width), BF16),
+            pltpu.VMEM((count, SIDE, SIDE), BF16),
+            pltpu.VMEM((BLOCKS, SIDE * SIDE), BF16),
+            pltpu.VMEM((2, GROUP * STRIDE, SIDE), F32),
+            pltpu.SemaphoreType.DMA((steps + 1,)),
+            pltpu.SemaphoreType.DMA((steps + 1,)),
+        ],
         compiler_params=params(),
         cost_estimate=cost(0, 4 * count * SIDE * SIDE),
         name="place",
-    )(back, back)
+    )(back)
 
 
 def shift(array, by, steps):

time: 172 us -> 169 us (0.983)
  Pallas kernels: 43.1 us -> 40.6 us
    pallas_call x2, Pallas kernels: 9.54 us -> 7.35 us  [the longest x1 4.62 us: partial_sums(): pl.pallas_call(functools.partial(partial_kernel, steps), in_specs=[pl.Blo...]
where the time goes in v3:
time: 169 us; the launch traced here: 168 us
  blocking collectives  58.6 us (35%)
  Pallas kernels  40.6 us (24%)
  waiting for transfers between devices  34.6 us (20%)
  starting transfers between devices  28.9 us (17%)
  local copies, waits for them, and re-layouts  2.77 us (2%)
  other arithmetic  2.13 us (1%)
    all_to_all x1, blocking collectives, body(): back = lax.all_to_all(back, PLANE, split_axis=0, concat_axis=0, tiled=True)  41.2 us
    all_to_all x1, waiting for transfers between devices, body(): got = lax.all_to_all(sent, PLANE, split_axis=0, concat_axis=0, tiled=True)  23.8 us
    pallas_call x1, Pallas kernels, convolve(): pl.pallas_call(functools.partial(conv_kernel, nb, (width - 1) // 2), grid...  21.4 us
    all_gather x1, blocking collectives, body(): coadd = lax.all_gather(own, FAR, axis=0, tiled=True)  17.4 us
    ppermute x3, waiting for transfers between devices, shift(): lax.ppermute(array, FAR, [(i, (i + by) % steps) for i in range(steps)])  10.7 us
    all_to_all x1, starting transfers between devices, body(): info = lax.all_to_all(info, PLANE, split_axis=0, concat_axis=0, tiled=True)  10.4 us
    ppermute x3, starting transfers between devices, shift(): lax.ppermute(array, FAR, [(i, (i + by) % steps) for i in range(steps)])  9.59 us
    all_to_all x1, starting transfers between devices, body(): got = lax.all_to_all(sent, PLANE, split_axis=0, concat_axis=0, tiled=True)  8.88 us
  transfers between devices with their start and end apart: 5, of which 4 were waited for; matrix products, arithmetic and copies ran while one was open for 1% of the time, Pallas kernels for 15%

profile of v3, /device:TPU:1, one launch (start us, length us, event | category | flops | bytes accessed | tf_op | source)
XLA Modules:
  0.0 168.4 jit_solution(1580263726827551201)
XLA Ops:
  0.6 0.7 pad_convert_fusion
  1.3 0.7 fusion
  2.0 0.8 broadcast_select_fusion
  2.8 10.4 %all-to-all-start = ((f32[64,8,128]{2,1,0:T(8,128)}), f32[64,8,128]{2,1,0:T(8,128)S(1)}, u32[]{:S(2)}, u32[]{:S(2)}) async-start(f32[64,8,128]{2,1,0:T(8,128)} %broadcast_select_fusion), calls=%async_computation | async-start | bytes 524288 | tf_op jit(solution)/shard_map/all_to_all | solution.py:311
  13.2 1.4 copy.9.coef_ref
  14.6 21.4 %convolve.1 = bf16[64,64,256]{2,1,0:T(8,128)(2,1)} custom-call(f32[64,21]{1,0:T(8,128)} %copy.9.coef_ref, bf16[64,128,128]{2,1,0:T(8,128)(2,1)} %x_ref.1, bf16[21,41]{1,0:T(8,128)(2,1)} %col_taps_ref.1, bf16[21,41]{1,0:T(8,128)(2,1)} %row_taps_ref.1), custom_call_target="tpu_custom_call" | custom-call | flops 11274289152 | bytes 4194304 | tf_op jit(solution)/shard_map/convolve/pallas_call | solution.py:79
  36.1 0.0 all-to-all-done.info_ref
  36.1 0.0 copy-start
  36.1 0.7 copy-done
  36.8 8.9 %all-to-all-start.1 = ((bf16[64,64,256]{2,1,0:T(8,128)(2,1)}), bf16[64,64,256]{2,1,0:T(8,128)(2,1)}, u32[]{:S(2)}, u32[]{:S(2)}) async-start(bf16[64,64,256]{2,1,0:T(8,128)(2,1)} %convolve.1), calls=%async_computation.1 | async-start | bytes 4194304 | tf_op jit(solution)/shard_map/all_to_all | solution.py:314
  45.7 4.1 %describe.1 = (f32[8,4096]{1,0:T(8,128)}, bf16[64,256]{1,0:T(8,128)(2,1)}) custom-call(s32[1]{0:T(128)} %bitcast.z_ref, f32[64,8,128]{2,1,0:T(8,128)} %copy-done), custom_call_target="tpu_custom_call" | custom-call | flops 16777216 | bytes 2097152 | tf_op jit(solution)/shard_map/describe/pallas_call | solution.py:130
  49.7 23.8 %all-to-all-done.1 = bf16[64,64,256]{2,1,0:T(8,128)(2,1)} async-done(((bf16[64,64,256]{2,1,0:T(8,128)(2,1)}), bf16[64,64,256]{2,1,0:T(8,128)(2,1)}, u32[]{:S(2)}, u32[]{:S(2)}) %all-to-all-start.1) | async-done | bytes 2097184 | tf_op jit(solution)/shard_map/all_to_all | solution.py:314
  73.6 4.6 %partial_sums.1 = (bf16[272,256]{1,0:T(8,128)(2,1)}, bf16[272,256]{1,0:T(8,128)(2,1)}, bf16[272,256]{1,0:T(8,128)(2,1)}, bf16[272,256]{1,0:T(8,128)(2,1)}) custom-call(s32[1]{0:T(128)} %bitcast.z_ref, f32[8,4096]{1,0:T(8,128)} %get-tuple-element.8.line_ref, bf16[4096,256]{1,0:T(8,128)(2,1)} %bitcast.2.got_ref, bf16[64,256]{1,0:T(8,128)(2,1)} %get-tuple-element.9.terms_ref), custom_call_target="tpu_custom_call" | custom-call | flops 2147483648 | bytes 2621440 | tf_op jit(solution)/shard_map/partial_sums/pallas_call | solution.py:157
  78.2 6.0 %collective-permute-start = (bf16[272,256]{1,0:T(8,128)(2,1)}, bf16[272,256]{1,0:T(8,128)(2,1)S(1)}, u32[]{:S(2)}, u32[]{:S(2)}) collective-permute-start(bf16[272,256]{1,0:T(8,128)(2,1)} %get-tuple-element.11), channel_id=1, source_target_pairs={{0,32},{16,48},{32,0},{48,16},{1,33},{17,49},{33,1},{49,17},{2,34}... | collective-permute-start | bytes 417800 | tf_op jit(solution)/shard_map/ppermute | solution.py:295
  84.2 1.2 collective-permute-start.1
  85.4 2.4 %collective-permute-start.2 = (bf16[272,256]{1,0:T(8,128)(2,1)}, bf16[272,256]{1,0:T(8,128)(2,1)S(1)}, u32[]{:S(2)}, u32[]{:S(2)}) collective-permute-start(bf16[272,256]{1,0:T(8,128)(2,1)} %get-tuple-element.13), channel_id=1, source_target_pairs={{0,48},{16,0},{32,16},{48,32},{1,49},{17,1},{33,17},{49,33},{2,50}... | collective-permute-start | bytes 417800 | tf_op jit(solution)/shard_map/ppermute | solution.py:295
  87.8 0.5 collective-permute-done.refs_1_
  88.2 0.0 copy-start.1
  88.2 7.9 %collective-permute-done.1.refs_2_ = bf16[272,256]{1,0:T(8,128)(2,1)S(1)} collective-permute-done((bf16[272,256]{1,0:T(8,128)(2,1)}, bf16[272,256]{1,0:T(8,128)(2,1)S(1)}, u32[]{:S(2)}, u32[]{:S(2)}) %collective-permute-start.1) | collective-permute-done | bytes 139296 | tf_op jit(solution)/shard_map/ppermute | solution.py:295
  96.1 0.0 copy-start.2
  96.1 2.4 %collective-permute-done.2.refs_3_ = bf16[272,256]{1,0:T(8,128)(2,1)S(1)} collective-permute-done((bf16[272,256]{1,0:T(8,128)(2,1)}, bf16[272,256]{1,0:T(8,128)(2,1)S(1)}, u32[]{:S(2)}, u32[]{:S(2)}) %collective-permute-start.2) | collective-permute-done | bytes 139296 | tf_op jit(solution)/shard_map/ppermute | solution.py:295
  98.5 0.0 copy-start.3
  98.5 0.0 copy-done.1
  98.5 0.0 copy-done.2
  98.5 0.7 copy-done.3
  99.2 1.9 %average.1.own_ref = bf16[256,256]{1,0:T(8,128)(2,1)} custom-call(bf16[272,256]{1,0:T(8,128)(2,1)} %get-tuple-element.10.refs_0_, bf16[272,256]{1,0:T(8,128)(2,1)} %copy-done.1, bf16[272,256]{1,0:T(8,128)(2,1)} %copy-done.2, bf16[272,256]{1,0:T(8,128)(2,1)} %copy-done.3), custom_call_target="tpu_custom_call" | custom-call | flops 655360 | bytes 1179648 | tf_op jit(solution)/shard_map/average/pallas_call | solution.py:182
  101.0 17.4 %all_gather.3.coadd_ref = bf16[1024,256]{1,0:T(8,128)(2,1)} all-gather(bf16[256,256]{1,0:T(8,128)(2,1)} %average.1.own_ref), channel_id=1, replica_groups=mesh['y'=4,'far'=4,'near'=2,'x'=4,'c'=2] {'far'}, dimensions={0}, use_global_device_ids=true | all-gather | bytes 655360 | tf_op jit(solution)/shard_map/all_gather | solution.py:320
  118.5 5.9 %subtract.1 = bf16[64,80,256]{2,1,0:T(8,128)(2,1)} custom-call(f32[8,4096]{1,0:T(8,128)} %get-tuple-element.8.line_ref, bf16[4096,256]{1,0:T(8,128)(2,1)} %bitcast.2.got_ref, bf16[1024,256]{1,0:T(8,128)(2,1)} %all_gather.3.coadd_ref, bf16[256,256]{1,0:T(8,128)(2,1)} %average.1.own_ref), custom_call_target="tpu_custom_call" | custom-call | flops 2147483648 | bytes 4718592 | tf_op jit(solution)/shard_map/subtract/pallas_call | solution.py:219
  124.4 41.2 %all_to_all.15.back_ref = bf16[64,80,256]{2,1,0:T(8,128)(2,1)} all-to-all(bf16[64,80,256]{2,1,0:T(8,128)(2,1)} %subtract.1), channel_id=1, replica_groups=mesh['y'=4,'far'=4,'near'=2,'x'=4,'c'=2] {'c','x','near','y'}, dimensions={0} | all-to-all | bytes 5242880 | tf_op jit(solution)/shard_map/all_to_all | solution.py:322
  165.6 2.7 %place.1 = (bf16[64,128,128]{2,1,0:T(8,128)(2,1)}, bf16[16,16384]{1,0:T(8,128)(2,1)}) custom-call(bf16[64,80,256]{2,1,0:T(8,128)(2,1)} %all_to_all.15.back_ref), custom_call_target="tpu_custom_call" | custom-call | bytes 4194304 | tf_op jit(solution)/shard_map/place/pallas_call | solution.py:271
  (2 shorter events, 0.0 us)
Async XLA Ops:
  2.8 33.3 %all-to-all-start = ((f32[64,8,128]{2,1,0:T(8,128)}), f32[64,8,128]{2,1,0:T(8,128)S(1)}, u32[]{:S(2)}, u32[]{:S(2)}) async-start(f32[64,8,128]{2,1,0:T(8,128)} %broadcast_select_fusion), calls=%async_computation | async-start | bytes 524288 | tf_op jit(solution)/shard_map/all_to_all | solution.py:311
  36.1 0.7 copy-start
  36.8 36.8 %all-to-all-start.1 = ((bf16[64,64,256]{2,1,0:T(8,128)(2,1)}), bf16[64,64,256]{2,1,0:T(8,128)(2,1)}, u32[]{:S(2)}, u32[]{:S(2)}) async-start(bf16[64,64,256]{2,1,0:T(8,128)(2,1)} %convolve.1), calls=%async_computation.1 | async-start | bytes 4194304 | tf_op jit(solution)/shard_map/all_to_all | solution.py:314
  78.2 10.0 %collective-permute-start = (bf16[272,256]{1,0:T(8,128)(2,1)}, bf16[272,256]{1,0:T(8,128)(2,1)S(1)}, u32[]{:S(2)}, u32[]{:S(2)}) collective-permute-start(bf16[272,256]{1,0:T(8,128)(2,1)} %get-tuple-element.11), channel_id=1, source_target_pairs={{0,32},{16,48},{32,0},{48,16},{1,33},{17,49},{33,1},{49,17},{2,34}... | collective-permute-start | bytes 417800 | tf_op jit(solution)/shard_map/ppermute | solution.py:295
  84.2 11.9 %collective-permute-start.1 = (bf16[272,256]{1,0:T(8,128)(2,1)}, bf16[272,256]{1,0:T(8,128)(2,1)S(1)}, u32[]{:S(2)}, u32[]{:S(2)}) collective-permute-start(bf16[272,256]{1,0:T(8,128)(2,1)} %get-tuple-element.12), channel_id=1, source_target_pairs={{0,16},{16,32},{32,48},{48,0},{1,17},{17,33},{33,49},{49,1},{2,18}... | collective-permute-start | bytes 417800 | tf_op jit(solution)/shard_map/ppermute | solution.py:295
  85.4 13.1 %collective-permute-start.2 = (bf16[272,256]{1,0:T(8,128)(2,1)}, bf16[272,256]{1,0:T(8,128)(2,1)S(1)}, u32[]{:S(2)}, u32[]{:S(2)}) collective-permute-start(bf16[272,256]{1,0:T(8,128)(2,1)} %get-tuple-element.13), channel_id=1, source_target_pairs={{0,48},{16,0},{32,16},{48,32},{1,49},{17,1},{33,17},{49,33},{2,50}... | collective-permute-start | bytes 417800 | tf_op jit(solution)/shard_map/ppermute | solution.py:295
  88.2 10.3 %copy-start.1 = (bf16[272,256]{1,0:T(8,128)(2,1)}, bf16[272,256]{1,0:T(8,128)(2,1)S(1)}, u32[]{:S(2)}) copy-start(bf16[272,256]{1,0:T(8,128)(2,1)S(1)} %collective-permute-done.refs_1_) | copy-start | bytes 417796
  96.1 2.4 %copy-start.2 = (bf16[272,256]{1,0:T(8,128)(2,1)}, bf16[272,256]{1,0:T(8,128)(2,1)S(1)}, u32[]{:S(2)}) copy-start(bf16[272,256]{1,0:T(8,128)(2,1)S(1)} %collective-permute-done.1.refs_2_) | copy-start | bytes 417796
  98.5 0.7 copy-start.3

commit v4 on v3

--- a/solution.py
+++ b/solution.py
@@ -20,7 +20,7 @@
 F32 = jnp.float32
 
 
-def params(limit=63 << 20):
+def params(limit=30 << 20):
     return pltpu.CompilerParams(vmem_limit_bytes=limit)
 
 
@@ -94,7 +94,7 @@
             pltpu.VMEM((GROUP // 2, nb * SIDE, 2 * SIDE), BF16),
             pltpu.VMEM((GROUP * STRIDE, SIDE), F32),
         ],
-        compiler_params=params(),
+        compiler_params=params(63 << 20),
         cost_estimate=cost(count * nb * SIDE**3 * 4, count * SIDE * SIDE * 4),
         name="convolve",
     )(coeffs, pieces, col_taps, row_taps)
@@ -215,7 +215,7 @@
 def subtract(lines, got, coadd, own, count, sizes):
     held, width = got.shape
     sources = held // count
-    some = 32
+    some = 64
     return pl.pallas_call(
         functools.partial(subtract_kernel, count, sizes),
         grid=(sources // some,),

time: 169 us -> 157 us (0.929)
  Pallas kernels: 40.6 us -> 30.6 us
  blocking collectives: 58.6 us -> 56.8 us
    pallas_call x1, Pallas kernels: 5.89 us -> 2.4 us  [subtract(): pl.pallas_call(functools.partial(subtract_kernel, count, sizes), grid=(so...]
    all_gather x1, blocking collectives: 17.4 us -> 14.6 us  [body(): coadd = lax.all_gather(own, FAR, axis=0, tiled=True)]
    pallas_call x1, Pallas kernels: 4.62 us -> 2.32 us  [partial_sums(): pl.pallas_call(functools.partial(partial_kernel, steps), in_specs=[pl.Blo...]
    pallas_call x1, Pallas kernels: 1.88 us -> 0.12 us  [average(): pl.pallas_call(functools.partial(average_kernel, own_rows), in_specs=[vme...]
where the time goes in v4:
time: 157 us
  blocking collectives  56.8 us (36%)
  waiting for transfers between devices  36 us (23%)
  Pallas kernels  30.6 us (19%)
  starting transfers between devices  29 us (18%)
  other arithmetic  2.13 us (1%)
    all_to_all x1, blocking collectives, body(): back = lax.all_to_all(back, PLANE, split_axis=0, concat_axis=0, tiled=True)  42.1 us
    all_to_all x1, waiting for transfers between devices, body(): got = lax.all_to_all(sent, PLANE, split_axis=0, concat_axis=0, tiled=True)  25.5 us
    pallas_call x1, Pallas kernels, convolve(): pl.pallas_call(functools.partial(conv_kernel, nb, (width - 1) // 2), grid...  21.4 us
    all_gather x1, blocking collectives, body(): coadd = lax.all_gather(own, FAR, axis=0, tiled=True)  14.6 us
    ppermute x3, waiting for transfers between devices, shift(): lax.ppermute(array, FAR, [(i, (i + by) % steps) for i in range(steps)])  10.5 us
    all_to_all x1, starting transfers between devices, body(): info = lax.all_to_all(info, PLANE, split_axis=0, concat_axis=0, tiled=True)  10.4 us
    ppermute x3, starting transfers between devices, shift(): lax.ppermute(array, FAR, [(i, (i + by) % steps) for i in range(steps)])  9.86 us
    all_to_all x1, starting transfers between devices, body(): got = lax.all_to_all(sent, PLANE, split_axis=0, concat_axis=0, tiled=True)  8.7 us
  transfers between devices with their start and end apart: 5, of which 4 were waited for; matrix products, arithmetic and copies ran while one was open for 1% of the time, Pallas kernels for 15%

profile of v4, /device:TPU:1, one launch (start us, length us, event | category | flops | bytes accessed | tf_op | source)
XLA Modules:
  0.0 156.8 jit_solution(15900083014461376659)
XLA Ops:
  0.6 0.7 pad_convert_fusion
  1.3 0.7 fusion
  2.0 0.8 broadcast_select_fusion
  2.8 10.4 %all-to-all-start = ((f32[64,8,128]{2,1,0:T(8,128)}), f32[64,8,128]{2,1,0:T(8,128)S(1)}, u32[]{:S(2)}, u32[]{:S(2)}) async-start(f32[64,8,128]{2,1,0:T(8,128)} %broadcast_select_fusion), calls=%async_computation | async-start | bytes 524288 | tf_op jit(solution)/shard_map/all_to_all | solution.py:311
  13.2 1.4 copy.9.coef_ref
  14.6 21.4 %convolve.1 = bf16[64,64,256]{2,1,0:T(8,128)(2,1)} custom-call(f32[64,21]{1,0:T(8,128)} %copy.9.coef_ref, bf16[64,128,128]{2,1,0:T(8,128)(2,1)} %x_ref.1, bf16[21,41]{1,0:T(8,128)(2,1)} %col_taps_ref.1, bf16[21,41]{1,0:T(8,128)(2,1)} %row_taps_ref.1), custom_call_target="tpu_custom_call" | custom-call | flops 11274289152 | bytes 4194304 | tf_op jit(solution)/shard_map/convolve/pallas_call | solution.py:79
  36.1 0.0 all-to-all-done.info_ref
  36.1 8.7 %all-to-all-start.1 = ((bf16[64,64,256]{2,1,0:T(8,128)(2,1)}), bf16[64,64,256]{2,1,0:T(8,128)(2,1)S(1)}, u32[]{:S(2)}, u32[]{:S(2)}) async-start(bf16[64,64,256]{2,1,0:T(8,128)(2,1)} %convolve.1), calls=%async_computation.1 | async-start | bytes 4194304 | tf_op jit(solution)/shard_map/all_to_all | solution.py:314
  44.8 2.5 %describe.1 = (f32[8,4096]{1,0:T(8,128)S(1)}, bf16[64,256]{1,0:T(8,128)(2,1)S(1)}) custom-call(s32[1]{0:T(128)} %bitcast.z_ref, f32[64,8,128]{2,1,0:T(8,128)S(1)} %all-to-all-done.info_ref), custom_call_target="tpu_custom_call" | custom-call | flops 16777216 | bytes 2097152 | tf_op jit(solution)/shard_map/describe/pallas_call | solution.py:130
  47.2 25.5 %all-to-all-done.1 = bf16[64,64,256]{2,1,0:T(8,128)(2,1)S(1)} async-done(((bf16[64,64,256]{2,1,0:T(8,128)(2,1)}), bf16[64,64,256]{2,1,0:T(8,128)(2,1)S(1)}, u32[]{:S(2)}, u32[]{:S(2)}) %all-to-all-start.1) | async-done | bytes 2097184 | tf_op jit(solution)/shard_map/all_to_all | solution.py:314
  72.8 2.3 %partial_sums.1 = (bf16[272,256]{1,0:T(8,128)(2,1)S(1)}, bf16[272,256]{1,0:T(8,128)(2,1)S(1)}, bf16[272,256]{1,0:T(8,128)(2,1)S(1)}, bf16[272,256]{1,0:T(8,128)(2,1)S(1)}) custom-call(s32[1]{0:T(128)} %bitcast.z_ref, f32[8,4096]{1,0:T(8,128)S(1)} %get-tuple-element.8.line_ref, bf16[4096,256]{1,0:T(8,128)(2,1)S(1)} %bitcast.6, ...), custom_call_target="tpu_custom_call" | custom-call | flops 2147483648 | bytes 2621440 | tf_op jit(solution)/shard_map/partial_sums/pallas_call | solution.py:157
  75.1 6.3 %collective-permute-start = (bf16[272,256]{1,0:T(8,128)(2,1)S(1)}, bf16[272,256]{1,0:T(8,128)(2,1)S(1)}, u32[]{:S(2)}, u32[]{:S(2)}) collective-permute-start(bf16[272,256]{1,0:T(8,128)(2,1)S(1)} %get-tuple-element.11), channel_id=1, source_target_pairs={{0,32},{16,48},{32,0},{48,16},{1,33},{17,49},{33,1},{49,17},{2,34}... | collective-permute-start | bytes 417800 | tf_op jit(solution)/shard_map/ppermute | solution.py:295
  81.4 1.2 collective-permute-start.1
  82.6 2.4 %collective-permute-start.2 = (bf16[272,256]{1,0:T(8,128)(2,1)S(1)}, bf16[272,256]{1,0:T(8,128)(2,1)S(1)}, u32[]{:S(2)}, u32[]{:S(2)}) collective-permute-start(bf16[272,256]{1,0:T(8,128)(2,1)S(1)} %get-tuple-element.13), channel_id=1, source_target_pairs={{0,48},{16,0},{32,16},{48,32},{1,49},{17,1},{33,17},{49,33},{2,50}... | collective-permute-start | bytes 417800 | tf_op jit(solution)/shard_map/ppermute | solution.py:295
  85.0 0.2 collective-permute-done.refs_1_
  85.2 7.8 %collective-permute-done.1.refs_2_ = bf16[272,256]{1,0:T(8,128)(2,1)S(1)} collective-permute-done((bf16[272,256]{1,0:T(8,128)(2,1)S(1)}, bf16[272,256]{1,0:T(8,128)(2,1)S(1)}, u32[]{:S(2)}, u32[]{:S(2)}) %collective-permute-start.1) | collective-permute-done | bytes 139296 | tf_op jit(solution)/shard_map/ppermute | solution.py:295
  93.0 2.4 %collective-permute-done.2.refs_3_ = bf16[272,256]{1,0:T(8,128)(2,1)S(1)} collective-permute-done((bf16[272,256]{1,0:T(8,128)(2,1)S(1)}, bf16[272,256]{1,0:T(8,128)(2,1)S(1)}, u32[]{:S(2)}, u32[]{:S(2)}) %collective-permute-start.2) | collective-permute-done | bytes 139296 | tf_op jit(solution)/shard_map/ppermute | solution.py:295
  95.5 0.1 average.1.own_ref
  95.6 14.6 %all_gather.3.coadd_ref = bf16[1024,256]{1,0:T(8,128)(2,1)S(1)} all-gather(bf16[256,256]{1,0:T(8,128)(2,1)S(1)} %average.1.own_ref), channel_id=1, replica_groups=mesh['y'=4,'far'=4,'near'=2,'x'=4,'c'=2] {'far'}, dimensions={0}, use_global_device_ids=true | all-gather | bytes 655360 | tf_op jit(solution)/shard_map/all_gather | solution.py:320
  110.2 2.4 %subtract.1 = bf16[64,80,256]{2,1,0:T(8,128)(2,1)S(1)} custom-call(f32[8,4096]{1,0:T(8,128)S(1)} %get-tuple-element.8.line_ref, bf16[4096,256]{1,0:T(8,128)(2,1)S(1)} %bitcast.7, bf16[1024,256]{1,0:T(8,128)(2,1)S(1)} %all_gather.3.coadd_ref, bf16[256,256]{1,0:T(8,128)(2,1)S(1)} %average.1.own_ref), custom_call_target="tpu_custom_call" | custom-call | flops 2147483648 | bytes 4718592 | tf_op jit(solution)/shard_map/subtract/pallas_call | solution.py:219
  112.6 42.1 %all_to_all.15.back_ref = bf16[64,80,256]{2,1,0:T(8,128)(2,1)S(1)} all-to-all(bf16[64,80,256]{2,1,0:T(8,128)(2,1)S(1)} %subtract.1), channel_id=1, replica_groups=mesh['y'=4,'far'=4,'near'=2,'x'=4,'c'=2] {'c','x','near','y'}, dimensions={0} | all-to-all | bytes 5242880 | tf_op jit(solution)/shard_map/all_to_all | solution.py:322
  154.8 1.9 %place.1 = (bf16[64,128,128]{2,1,0:T(8,128)(2,1)}, bf16[16,16384]{1,0:T(8,128)(2,1)}) custom-call(bf16[64,80,256]{2,1,0:T(8,128)(2,1)S(1)} %all_to_all.15.back_ref), custom_call_target="tpu_custom_call" | custom-call | bytes 4194304 | tf_op jit(solution)/shard_map/place/pallas_call | solution.py:271
  (2 shorter events, 0.0 us)
Async XLA Ops:
  2.8 33.3 %all-to-all-start = ((f32[64,8,128]{2,1,0:T(8,128)}), f32[64,8,128]{2,1,0:T(8,128)S(1)}, u32[]{:S(2)}, u32[]{:S(2)}) async-start(f32[64,8,128]{2,1,0:T(8,128)} %broadcast_select_fusion), calls=%async_computation | async-start | bytes 524288 | tf_op jit(solution)/shard_map/all_to_all | solution.py:311
  36.1 36.7 %all-to-all-start.1 = ((bf16[64,64,256]{2,1,0:T(8,128)(2,1)}), bf16[64,64,256]{2,1,0:T(8,128)(2,1)S(1)}, u32[]{:S(2)}, u32[]{:S(2)}) async-start(bf16[64,64,256]{2,1,0:T(8,128)(2,1)} %convolve.1), calls=%async_computation.1 | async-start | bytes 4194304 | tf_op jit(solution)/shard_map/all_to_all | solution.py:314
  75.1 10.1 %collective-permute-start = (bf16[272,256]{1,0:T(8,128)(2,1)S(1)}, bf16[272,256]{1,0:T(8,128)(2,1)S(1)}, u32[]{:S(2)}, u32[]{:S(2)}) collective-permute-start(bf16[272,256]{1,0:T(8,128)(2,1)S(1)} %get-tuple-element.11), channel_id=1, source_target_pairs={{0,32},{16,48},{32,0},{48,16},{1,33},{17,49},{33,1},{49,17},{2,34}... | collective-permute-start | bytes 417800 | tf_op jit(solution)/shard_map/ppermute | solution.py:295
  81.4 11.7 %collective-permute-start.1 = (bf16[272,256]{1,0:T(8,128)(2,1)S(1)}, bf16[272,256]{1,0:T(8,128)(2,1)S(1)}, u32[]{:S(2)}, u32[]{:S(2)}) collective-permute-start(bf16[272,256]{1,0:T(8,128)(2,1)S(1)} %get-tuple-element.12), channel_id=1, source_target_pairs={{0,16},{16,32},{32,48},{48,0},{1,17},{17,33},{33,49},{49,1},{2,18}... | collective-permute-start | bytes 417800 | tf_op jit(solution)/shard_map/ppermute | solution.py:295
  82.6 12.9 %collective-permute-start.2 = (bf16[272,256]{1,0:T(8,128)(2,1)S(1)}, bf16[272,256]{1,0:T(8,128)(2,1)S(1)}, u32[]{:S(2)}, u32[]{:S(2)}) collective-permute-start(bf16[272,256]{1,0:T(8,128)(2,1)S(1)} %get-tuple-element.13), channel_id=1, source_target_pairs={{0,48},{16,0},{32,16},{48,32},{1,49},{17,1},{33,17},{49,33},{2,50}... | collective-permute-start | bytes 417800 | tf_op jit(solution)/shard_map/ppermute | solution.py:295

commit v5 on v4

--- a/solution.py
+++ b/solution.py
@@ -14,7 +14,7 @@
 TAIL = 16
 STRIDE = 132
 FAR = "far"
-PLANE = ("c", "x", "near", "y")
+PLANE = ("c", "y", "x", "near")
 EVERY = ("y", "far", "near", "x", "c")
 BF16 = jnp.bfloat16
 F32 = jnp.float32
@@ -36,11 +36,13 @@
     return jnp.where(jnp.abs(columns - rows) <= half, moved, 0.0)
 
 
-def conv_kernel(nb, half, coef_ref, x_ref, col_taps_ref, row_taps_ref, out_ref, col_ref, row_ref, taps_ref, z_ref, m_ref):
+def conv_kernel(nb, half, coeffs_ref, x_ref, col_taps_ref, row_taps_ref, out_ref, coef_ref, col_ref, row_ref, taps_ref, z_ref, m_ref, sem):
     step = pl.program_id(0)
 
     @pl.when(step == 0)
     def _():
+        copy = pltpu.make_async_copy(coeffs_ref, coef_ref, sem)
+        copy.start()
         for source, target, flip in ((col_taps_ref, col_ref, True), (row_taps_ref, row_ref, False)):
             taps_ref[...] = jnp.zeros_like(taps_ref)
             taps_ref[:nb, : 2 * half + 1] = source[...].astype(F32)
@@ -49,6 +51,7 @@
                 matrix = band(taps_ref, b, half)
                 matrix = matrix.T if flip else matrix
                 target[:, b * SIDE : (b + 1) * SIDE] = matrix.astype(BF16)
+        copy.wait()
 
     x = x_ref[...].reshape(GROUP * SIDE, SIDE)
     for first in range(0, nb, 2):
@@ -59,7 +62,7 @@
             for p in range(GROUP):
                 part = inner[p * SIDE : (p + 1) * SIDE, k * SIDE : (k + 1) * SIDE]
                 z_ref[p // 2, b * SIDE : (b + 1) * SIDE, (p % 2) * SIDE : (p % 2 + 1) * SIDE] = (
-                    part * coef_ref[step * GROUP + p, b]
+                    part * coef_ref[b, step * GROUP + p]
                 ).astype(BF16)
     for pair in range(GROUP // 2):
         outer = jnp.dot(row_ref[...], z_ref[pair], preferred_element_type=F32)
@@ -80,7 +83,7 @@
         functools.partial(conv_kernel, nb, (width - 1) // 2),
         grid=(count // GROUP,),
         in_specs=[
-            pl.BlockSpec(memory_space=pltpu.SMEM),
+            pl.BlockSpec(memory_space=pl.ANY),
             pl.BlockSpec((GROUP, SIDE, SIDE), lambda g: (g, 0, 0)),
             pl.BlockSpec((nb, width), lambda g: (0, 0)),
             pl.BlockSpec((nb, width), lambda g: (0, 0)),
@@ -88,16 +91,18 @@
         out_specs=pl.BlockSpec((chunks, GROUP, SIDE * SIDE // chunks), lambda g: (0, g, 0)),
         out_shape=jax.ShapeDtypeStruct((chunks, count, SIDE * SIDE // chunks), BF16),
         scratch_shapes=[
+            pltpu.SMEM(coeffs.shape[::-1], F32),
             pltpu.VMEM((SIDE, nb * SIDE), BF16),
             pltpu.VMEM((SIDE, nb * SIDE), BF16),
             pltpu.VMEM((padded, SIDE), F32),
             pltpu.VMEM((GROUP // 2, nb * SIDE, 2 * SIDE), BF16),
             pltpu.VMEM((GROUP * STRIDE, SIDE), F32),
+            pltpu.SemaphoreType.DMA(()),
         ],
         compiler_params=params(63 << 20),
         cost_estimate=cost(count * nb * SIDE**3 * 4, count * SIDE * SIDE * 4),
         name="convolve",
-    )(coeffs, pieces, col_taps, row_taps)
+    )(coeffs.T, pieces, col_taps, row_taps)
 
 
 def describe_kernel(steps, own_rows, z_ref, info_ref, line_ref, out_ref):
@@ -201,13 +206,13 @@
         marks.append(jnp.where(index == column, 1.0, 0.0).astype(BF16))
     under = jnp.dot(jnp.concatenate(marks), coadd_ref[...], preferred_element_type=F32)
     diff = (got_ref[...].astype(F32) - under).astype(BF16)
-    n_core, n_x, n_near, n_y = sizes
+    n_core, n_y, n_x, n_near = sizes
     for s in range(sources):
         out_ref[s, :count, :] = diff[s * count : (s + 1) * count]
         place = pl.program_id(0) * sources + s
-        near = lax.rem(place // n_y, n_near)
-        x = lax.rem(place // (n_y * n_near), n_x)
-        core = place // (n_y * n_near * n_x)
+        near = lax.rem(place, n_near)
+        x = lax.rem(place // n_near, n_x)
+        core = place // (n_near * n_x * n_y)
         first = pl.multiple_of(((near * n_x + x) * n_core + core) * BLOCKS, BLOCKS)
         out_ref[s, count:, :] = own_ref[pl.ds(first, BLOCKS), :]
 

time: 157 us -> 157 us (level)
  transfers between devices with their start and end apart: 5 -> 5, of which waited for: 4 -> 3; matrix products, arithmetic and copies ran while one was open for 1% -> 0% of each run, Pallas kernels for 15% -> 16%
where the time goes in v5:
time: 157 us
  blocking collectives  57.2 us (36%)
  waiting for transfers between devices  36.7 us (23%)
  Pallas kernels  31.1 us (20%)
  starting transfers between devices  29 us (18%)
  other arithmetic  2.13 us (1%)
    all_to_all x1, blocking collectives, body(): back = lax.all_to_all(back, PLANE, split_axis=0, concat_axis=0, tiled=True)  41.2 us
    all_to_all x1, waiting for transfers between devices, body(): got = lax.all_to_all(sent, PLANE, split_axis=0, concat_axis=0, tiled=True)  25.4 us
    pallas_call x1, Pallas kernels, convolve(): pl.pallas_call(functools.partial(conv_kernel, nb, (width - 1) // 2), grid...  21.9 us
    all_gather x1, blocking collectives, body(): coadd = lax.all_gather(own, FAR, axis=0, tiled=True)  16.1 us
    ppermute x3, waiting for transfers between devices, shift(): lax.ppermute(array, FAR, [(i, (i + by) % steps) for i in range(steps)])  11.3 us
    all_to_all x1, starting transfers between devices, body(): info = lax.all_to_all(info, PLANE, split_axis=0, concat_axis=0, tiled=True)  10.4 us
    ppermute x3, starting transfers between devices, shift(): lax.ppermute(array, FAR, [(i, (i + by) % steps) for i in range(steps)])  9.86 us
    all_to_all x1, starting transfers between devices, body(): got = lax.all_to_all(sent, PLANE, split_axis=0, concat_axis=0, tiled=True)  8.7 us
  transfers between devices with their start and end apart: 5, of which 3 were waited for; matrix products, arithmetic and copies ran while one was open for 0% of the time, Pallas kernels for 16%

profile of v5, /device:TPU:1, one launch (start us, length us, event | category | flops | bytes accessed | tf_op | source)
XLA Modules:
  0.0 157.0 jit_solution(4976234709853819190)
XLA Ops:
  0.6 0.7 pad_convert_fusion
  1.3 0.7 fusion
  2.0 0.8 broadcast_select_fusion
  2.8 10.4 %all-to-all-start = ((f32[64,8,128]{2,1,0:T(8,128)}), f32[64,8,128]{2,1,0:T(8,128)S(1)}, u32[]{:S(2)}, u32[]{:S(2)}) async-start(f32[64,8,128]{2,1,0:T(8,128)} %broadcast_select_fusion), calls=%async_computation | async-start | bytes 524288 | tf_op jit(solution)/shard_map/all_to_all | solution.py:316
  13.2 21.9 %convolve.1 = bf16[64,64,256]{2,1,0:T(8,128)(2,1)} custom-call(f32[21,64]{1,0:T(8,128)} %bitcast.9, bf16[64,128,128]{2,1,0:T(8,128)(2,1)} %x_ref.1, bf16[21,41]{1,0:T(8,128)(2,1)} %col_taps_ref.1, bf16[21,41]{1,0:T(8,128)(2,1)} %row_taps_ref.1), custom_call_target="tpu_custom_call" | custom-call | flops 11274289152 | bytes 4194304 | tf_op jit(solution)/shard_map/convolve/pallas_call | solution.py:82
  35.1 0.0 all-to-all-done.info_ref
  35.2 8.7 %all-to-all-start.1 = ((bf16[64,64,256]{2,1,0:T(8,128)(2,1)}), bf16[64,64,256]{2,1,0:T(8,128)(2,1)S(1)}, u32[]{:S(2)}, u32[]{:S(2)}) async-start(bf16[64,64,256]{2,1,0:T(8,128)(2,1)} %convolve.1), calls=%async_computation.1 | async-start | bytes 4194304 | tf_op jit(solution)/shard_map/all_to_all | solution.py:319
  43.9 2.5 %describe.1 = (f32[8,4096]{1,0:T(8,128)S(1)}, bf16[64,256]{1,0:T(8,128)(2,1)S(1)}) custom-call(s32[1]{0:T(128)} %bitcast.z_ref, f32[64,8,128]{2,1,0:T(8,128)S(1)} %all-to-all-done.info_ref), custom_call_target="tpu_custom_call" | custom-call | flops 16777216 | bytes 2097152 | tf_op jit(solution)/shard_map/describe/pallas_call | solution.py:135
  46.3 25.4 %all-to-all-done.1 = bf16[64,64,256]{2,1,0:T(8,128)(2,1)S(1)} async-done(((bf16[64,64,256]{2,1,0:T(8,128)(2,1)}), bf16[64,64,256]{2,1,0:T(8,128)(2,1)S(1)}, u32[]{:S(2)}, u32[]{:S(2)}) %all-to-all-start.1) | async-done | bytes 2097184 | tf_op jit(solution)/shard_map/all_to_all | solution.py:319
  71.8 2.3 %partial_sums.1 = (bf16[272,256]{1,0:T(8,128)(2,1)S(1)}, bf16[272,256]{1,0:T(8,128)(2,1)S(1)}, bf16[272,256]{1,0:T(8,128)(2,1)S(1)}, bf16[272,256]{1,0:T(8,128)(2,1)S(1)}) custom-call(s32[1]{0:T(128)} %bitcast.z_ref, f32[8,4096]{1,0:T(8,128)S(1)} %get-tuple-element.8.line_ref, bf16[4096,256]{1,0:T(8,128)(2,1)S(1)} %bitcast.7, ...), custom_call_target="tpu_custom_call" | custom-call | flops 2147483648 | bytes 2621440 | tf_op jit(solution)/shard_map/partial_sums/pallas_call | solution.py:162
  74.1 6.3 %collective-permute-start = (bf16[272,256]{1,0:T(8,128)(2,1)S(1)}, bf16[272,256]{1,0:T(8,128)(2,1)S(1)}, u32[]{:S(2)}, u32[]{:S(2)}) collective-permute-start(bf16[272,256]{1,0:T(8,128)(2,1)S(1)} %get-tuple-element.11), channel_id=1, source_target_pairs={{0,32},{16,48},{32,0},{48,16},{1,33},{17,49},{33,1},{49,17},{2,34}... | collective-permute-start | bytes 417800 | tf_op jit(solution)/shard_map/ppermute | solution.py:300
  80.4 1.2 collective-permute-start.1
  81.6 2.4 %collective-permute-start.2 = (bf16[272,256]{1,0:T(8,128)(2,1)S(1)}, bf16[272,256]{1,0:T(8,128)(2,1)S(1)}, u32[]{:S(2)}, u32[]{:S(2)}) collective-permute-start(bf16[272,256]{1,0:T(8,128)(2,1)S(1)} %get-tuple-element.13), channel_id=1, source_target_pairs={{0,48},{16,0},{32,16},{48,32},{1,49},{17,1},{33,17},{49,33},{2,50}... | collective-permute-start | bytes 417800 | tf_op jit(solution)/shard_map/ppermute | solution.py:300
  83.9 0.0 collective-permute-done.refs_1_
  84.0 8.3 %collective-permute-done.1.refs_2_ = bf16[272,256]{1,0:T(8,128)(2,1)S(1)} collective-permute-done((bf16[272,256]{1,0:T(8,128)(2,1)S(1)}, bf16[272,256]{1,0:T(8,128)(2,1)S(1)}, u32[]{:S(2)}, u32[]{:S(2)}) %collective-permute-start.1) | collective-permute-done | bytes 139296 | tf_op jit(solution)/shard_map/ppermute | solution.py:300
  92.3 3.0 %collective-permute-done.2.refs_3_ = bf16[272,256]{1,0:T(8,128)(2,1)S(1)} collective-permute-done((bf16[272,256]{1,0:T(8,128)(2,1)S(1)}, bf16[272,256]{1,0:T(8,128)(2,1)S(1)}, u32[]{:S(2)}, u32[]{:S(2)}) %collective-permute-start.2) | collective-permute-done | bytes 139296 | tf_op jit(solution)/shard_map/ppermute | solution.py:300
  95.2 0.1 average.1.own_ref
  95.4 16.1 %all_gather.3.coadd_ref = bf16[1024,256]{1,0:T(8,128)(2,1)S(1)} all-gather(bf16[256,256]{1,0:T(8,128)(2,1)S(1)} %average.1.own_ref), channel_id=1, replica_groups=mesh['y'=4,'far'=4,'near'=2,'x'=4,'c'=2] {'far'}, dimensions={0}, use_global_device_ids=true | all-gather | bytes 655360 | tf_op jit(solution)/shard_map/all_gather | solution.py:325
  111.4 2.4 %subtract.1 = bf16[64,80,256]{2,1,0:T(8,128)(2,1)S(1)} custom-call(f32[8,4096]{1,0:T(8,128)S(1)} %get-tuple-element.8.line_ref, bf16[4096,256]{1,0:T(8,128)(2,1)S(1)} %bitcast.8, bf16[1024,256]{1,0:T(8,128)(2,1)S(1)} %all_gather.3.coadd_ref, bf16[256,256]{1,0:T(8,128)(2,1)S(1)} %average.1.own_ref), custom_call_target="tpu_custom_call" | custom-call | flops 2147483648 | bytes 4718592 | tf_op jit(solution)/shard_map/subtract/pallas_call | solution.py:224
  113.8 41.2 %all_to_all.15.back_ref = bf16[64,80,256]{2,1,0:T(8,128)(2,1)S(1)} all-to-all(bf16[64,80,256]{2,1,0:T(8,128)(2,1)S(1)} %subtract.1), channel_id=1, replica_groups=mesh['y'=4,'far'=4,'near'=2,'x'=4,'c'=2] {'c','y','x','near'}, dimensions={0} | all-to-all | bytes 5242880 | tf_op jit(solution)/shard_map/all_to_all | solution.py:327
  155.0 1.9 %place.1 = (bf16[64,128,128]{2,1,0:T(8,128)(2,1)}, bf16[16,16384]{1,0:T(8,128)(2,1)}) custom-call(bf16[64,80,256]{2,1,0:T(8,128)(2,1)S(1)} %all_to_all.15.back_ref), custom_call_target="tpu_custom_call" | custom-call | bytes 4194304 | tf_op jit(solution)/shard_map/place/pallas_call | solution.py:276
  (2 shorter events, 0.0 us)
Async XLA Ops:
  2.8 32.4 %all-to-all-start = ((f32[64,8,128]{2,1,0:T(8,128)}), f32[64,8,128]{2,1,0:T(8,128)S(1)}, u32[]{:S(2)}, u32[]{:S(2)}) async-start(f32[64,8,128]{2,1,0:T(8,128)} %broadcast_select_fusion), calls=%async_computation | async-start | bytes 524288 | tf_op jit(solution)/shard_map/all_to_all | solution.py:316
  35.2 36.6 %all-to-all-start.1 = ((bf16[64,64,256]{2,1,0:T(8,128)(2,1)}), bf16[64,64,256]{2,1,0:T(8,128)(2,1)S(1)}, u32[]{:S(2)}, u32[]{:S(2)}) async-start(bf16[64,64,256]{2,1,0:T(8,128)(2,1)} %convolve.1), calls=%async_computation.1 | async-start | bytes 4194304 | tf_op jit(solution)/shard_map/all_to_all | solution.py:319
  74.1 9.9 %collective-permute-start = (bf16[272,256]{1,0:T(8,128)(2,1)S(1)}, bf16[272,256]{1,0:T(8,128)(2,1)S(1)}, u32[]{:S(2)}, u32[]{:S(2)}) collective-permute-start(bf16[272,256]{1,0:T(8,128)(2,1)S(1)} %get-tuple-element.11), channel_id=1, source_target_pairs={{0,32},{16,48},{32,0},{48,16},{1,33},{17,49},{33,1},{49,17},{2,34}... | collective-permute-start | bytes 417800 | tf_op jit(solution)/shard_map/ppermute | solution.py:300
  80.4 11.9 %collective-permute-start.1 = (bf16[272,256]{1,0:T(8,128)(2,1)S(1)}, bf16[272,256]{1,0:T(8,128)(2,1)S(1)}, u32[]{:S(2)}, u32[]{:S(2)}) collective-permute-start(bf16[272,256]{1,0:T(8,128)(2,1)S(1)} %get-tuple-element.12), channel_id=1, source_target_pairs={{0,16},{16,32},{32,48},{48,0},{1,17},{17,33},{33,49},{49,1},{2,18}... | collective-permute-start | bytes 417800 | tf_op jit(solution)/shard_map/ppermute | solution.py:300
  81.6 13.7 %collective-permute-start.2 = (bf16[272,256]{1,0:T(8,128)(2,1)S(1)}, bf16[272,256]{1,0:T(8,128)(2,1)S(1)}, u32[]{:S(2)}, u32[]{:S(2)}) collective-permute-start(bf16[272,256]{1,0:T(8,128)(2,1)S(1)} %get-tuple-element.13), channel_id=1, source_target_pairs={{0,48},{16,0},{32,16},{48,32},{1,49},{17,1},{33,17},{49,33},{2,50}... | collective-permute-start | bytes 417800 | tf_op jit(solution)/shard_map/ppermute | solution.py:300

commit v6 on v5

--- a/solution.py
+++ b/solution.py
@@ -103,6 +103,29 @@
         cost_estimate=cost(count * nb * SIDE**3 * 4, count * SIDE * SIDE * 4),
         name="convolve",
     )(coeffs.T, pieces, col_taps, row_taps)
+
+
+def lines_kernel(owner_ref, block_ref, weight_ref, out_ref, tile_ref):
+    count = owner_ref.shape[1]
+    tile_ref[...] = jnp.zeros_like(tile_ref)
+    tile_ref[0:1, :count] = (owner_ref[...] * BLOCKS + block_ref[...]).astype(F32)
+    tile_ref[1:2, :count] = weight_ref[...].astype(F32)
+    out_ref[...] = jnp.broadcast_to(tile_ref[...][None], out_ref.shape)
+
+
+def make_lines(routes, blocks, weights, chunks):
+    count = blocks.shape[0]
+    vmem = pl.BlockSpec(memory_space=pltpu.VMEM)
+    return pl.pallas_call(
+        lines_kernel,
+        in_specs=[vmem] * 3,
+        out_specs=vmem,
+        out_shape=jax.ShapeDtypeStruct((chunks, HEAD, SIDE), F32),
+        scratch_shapes=[pltpu.VMEM((HEAD, SIDE), F32)],
+        compiler_params=params(63 << 20),
+        cost_estimate=cost(0, chunks * HEAD * SIDE * 4),
+        name="make_lines",
+    )(routes.T, blocks.reshape(1, count), weights.reshape(1, count))
 
 
 def describe_kernel(steps, own_rows, z_ref, info_ref, line_ref, out_ref):
@@ -309,10 +332,7 @@
     z = lax.axis_index(FAR).astype(jnp.int32).reshape(1)
     others = sorted(range(1, steps), key=lambda k: -min(k, steps - k))
 
-    row = jnp.pad((routes[:, 0] * BLOCKS + blocks).astype(F32), (0, SIDE - count))
-    weight = jnp.pad(weights.astype(F32), (0, SIDE - count))
-    line = lax.broadcasted_iota(jnp.int32, (chunks, HEAD, SIDE), 1)
-    info = jnp.where(line == 0, row, weight)
+    info = make_lines(routes, blocks, weights, chunks)
     info = lax.all_to_all(info, PLANE, split_axis=0, concat_axis=0, tiled=True)
 
     sent = convolve(pieces, coeffs, col_taps, row_taps, chunks)

time: 157 us -> 157 us (level)
  other arithmetic: 2.13 us -> 0 us
where the time goes in v6:
time: 157 us; the launch traced here: 156 us
  blocking collectives  57.2 us (36%)
  waiting for transfers between devices  36.7 us (23%)
  Pallas kernels  32.5 us (21%)
  starting transfers between devices  29 us (18%)
    all_to_all x1, blocking collectives, body(): back = lax.all_to_all(back, PLANE, split_axis=0, concat_axis=0, tiled=True)  41.2 us
    all_to_all x1, waiting for transfers between devices, body(): got = lax.all_to_all(sent, PLANE, split_axis=0, concat_axis=0, tiled=True)  25.4 us
    pallas_call x1, Pallas kernels, convolve(): pl.pallas_call(functools.partial(conv_kernel, nb, (width - 1) // 2), grid...  21.9 us
    all_gather x1, blocking collectives, body(): coadd = lax.all_gather(own, FAR, axis=0, tiled=True)  16.1 us
    ppermute x3, waiting for transfers between devices, shift(): lax.ppermute(array, FAR, [(i, (i + by) % steps) for i in range(steps)])  11.3 us
    all_to_all x1, starting transfers between devices, body(): info = lax.all_to_all(info, PLANE, split_axis=0, concat_axis=0, tiled=True)  10.4 us
    ppermute x3, starting transfers between devices, shift(): lax.ppermute(array, FAR, [(i, (i + by) % steps) for i in range(steps)])  9.85 us
    all_to_all x1, starting transfers between devices, body(): got = lax.all_to_all(sent, PLANE, split_axis=0, concat_axis=0, tiled=True)  8.67 us
  transfers between devices with their start and end apart: 5, of which 3 were waited for; matrix products, arithmetic and copies ran while one was open for 0% of the time, Pallas kernels for 16%

profile of v6, /device:TPU:1, one launch (start us, length us, event | category | flops | bytes accessed | tf_op | source)
XLA Modules:
  0.0 156.3 jit_solution(9731204634050322950)
XLA Ops:
  0.6 1.4 make_lines.1
  2.0 10.4 %all-to-all-start = ((f32[64,8,128]{2,1,0:T(8,128)}), f32[64,8,128]{2,1,0:T(8,128)S(1)}, u32[]{:S(2)}, u32[]{:S(2)}) async-start(f32[64,8,128]{2,1,0:T(8,128)} %make_lines.1), calls=%async_computation | async-start | bytes 524288 | tf_op jit(solution)/shard_map/all_to_all | solution.py:336
  12.5 21.9 %convolve.1 = bf16[64,64,256]{2,1,0:T(8,128)(2,1)} custom-call(f32[21,64]{1,0:T(8,128)} %bitcast.11, bf16[64,128,128]{2,1,0:T(8,128)(2,1)} %x_ref.1, bf16[21,41]{1,0:T(8,128)(2,1)} %col_taps_ref.1, bf16[21,41]{1,0:T(8,128)(2,1)} %row_taps_ref.1), custom_call_target="tpu_custom_call" | custom-call | flops 11274289152 | bytes 4194304 | tf_op jit(solution)/shard_map/convolve/pallas_call | solution.py:82
  34.4 0.0 all-to-all-done.info_ref
  34.5 8.7 %all-to-all-start.1 = ((bf16[64,64,256]{2,1,0:T(8,128)(2,1)}), bf16[64,64,256]{2,1,0:T(8,128)(2,1)S(1)}, u32[]{:S(2)}, u32[]{:S(2)}) async-start(bf16[64,64,256]{2,1,0:T(8,128)(2,1)} %convolve.1), calls=%async_computation.1 | async-start | bytes 4194304 | tf_op jit(solution)/shard_map/all_to_all | solution.py:339
  43.1 2.5 %describe.1 = (f32[8,4096]{1,0:T(8,128)S(1)}, bf16[64,256]{1,0:T(8,128)(2,1)S(1)}) custom-call(s32[1]{0:T(128)} %bitcast.z_ref, f32[64,8,128]{2,1,0:T(8,128)S(1)} %all-to-all-done.info_ref), custom_call_target="tpu_custom_call" | custom-call | flops 16777216 | bytes 2097152 | tf_op jit(solution)/shard_map/describe/pallas_call | solution.py:158
  45.6 25.4 %all-to-all-done.1 = bf16[64,64,256]{2,1,0:T(8,128)(2,1)S(1)} async-done(((bf16[64,64,256]{2,1,0:T(8,128)(2,1)}), bf16[64,64,256]{2,1,0:T(8,128)(2,1)S(1)}, u32[]{:S(2)}, u32[]{:S(2)}) %all-to-all-start.1) | async-done | bytes 2097184 | tf_op jit(solution)/shard_map/all_to_all | solution.py:339
  71.0 2.3 %partial_sums.1 = (bf16[272,256]{1,0:T(8,128)(2,1)S(1)}, bf16[272,256]{1,0:T(8,128)(2,1)S(1)}, bf16[272,256]{1,0:T(8,128)(2,1)S(1)}, bf16[272,256]{1,0:T(8,128)(2,1)S(1)}) custom-call(s32[1]{0:T(128)} %bitcast.z_ref, f32[8,4096]{1,0:T(8,128)S(1)} %get-tuple-element.8.line_ref, bf16[4096,256]{1,0:T(8,128)(2,1)S(1)} %bitcast.6, ...), custom_call_target="tpu_custom_call" | custom-call | flops 2147483648 | bytes 2621440 | tf_op jit(solution)/shard_map/partial_sums/pallas_call | solution.py:185
  73.4 6.3 %collective-permute-start = (bf16[272,256]{1,0:T(8,128)(2,1)S(1)}, bf16[272,256]{1,0:T(8,128)(2,1)S(1)}, u32[]{:S(2)}, u32[]{:S(2)}) collective-permute-start(bf16[272,256]{1,0:T(8,128)(2,1)S(1)} %get-tuple-element.11), channel_id=1, source_target_pairs={{0,32},{16,48},{32,0},{48,16},{1,33},{17,49},{33,1},{49,17},{2,34}... | collective-permute-start | bytes 417800 | tf_op jit(solution)/shard_map/ppermute | solution.py:323
  79.6 1.2 collective-permute-start.1
  80.8 2.4 %collective-permute-start.2 = (bf16[272,256]{1,0:T(8,128)(2,1)S(1)}, bf16[272,256]{1,0:T(8,128)(2,1)S(1)}, u32[]{:S(2)}, u32[]{:S(2)}) collective-permute-start(bf16[272,256]{1,0:T(8,128)(2,1)S(1)} %get-tuple-element.13), channel_id=1, source_target_pairs={{0,48},{16,0},{32,16},{48,32},{1,49},{17,1},{33,17},{49,33},{2,50}... | collective-permute-start | bytes 417800 | tf_op jit(solution)/shard_map/ppermute | solution.py:323
  83.2 0.0 collective-permute-done.refs_1_
  83.2 8.3 %collective-permute-done.1.refs_2_ = bf16[272,256]{1,0:T(8,128)(2,1)S(1)} collective-permute-done((bf16[272,256]{1,0:T(8,128)(2,1)S(1)}, bf16[272,256]{1,0:T(8,128)(2,1)S(1)}, u32[]{:S(2)}, u32[]{:S(2)}) %collective-permute-start.1) | collective-permute-done | bytes 139296 | tf_op jit(solution)/shard_map/ppermute | solution.py:323
  91.5 3.0 %collective-permute-done.2.refs_3_ = bf16[272,256]{1,0:T(8,128)(2,1)S(1)} collective-permute-done((bf16[272,256]{1,0:T(8,128)(2,1)S(1)}, bf16[272,256]{1,0:T(8,128)(2,1)S(1)}, u32[]{:S(2)}, u32[]{:S(2)}) %collective-permute-start.2) | collective-permute-done | bytes 139296 | tf_op jit(solution)/shard_map/ppermute | solution.py:323
  94.5 0.1 average.1.own_ref
  94.6 16.1 %all_gather.3.coadd_ref = bf16[1024,256]{1,0:T(8,128)(2,1)S(1)} all-gather(bf16[256,256]{1,0:T(8,128)(2,1)S(1)} %average.1.own_ref), channel_id=1, replica_groups=mesh['y'=4,'far'=4,'near'=2,'x'=4,'c'=2] {'far'}, dimensions={0}, use_global_device_ids=true | all-gather | bytes 655360 | tf_op jit(solution)/shard_map/all_gather | solution.py:345
  110.7 2.4 %subtract.1 = bf16[64,80,256]{2,1,0:T(8,128)(2,1)S(1)} custom-call(f32[8,4096]{1,0:T(8,128)S(1)} %get-tuple-element.8.line_ref, bf16[4096,256]{1,0:T(8,128)(2,1)S(1)} %bitcast.7, bf16[1024,256]{1,0:T(8,128)(2,1)S(1)} %all_gather.3.coadd_ref, bf16[256,256]{1,0:T(8,128)(2,1)S(1)} %average.1.own_ref), custom_call_target="tpu_custom_call" | custom-call | flops 2147483648 | bytes 4718592 | tf_op jit(solution)/shard_map/subtract/pallas_call | solution.py:247
  113.1 41.2 %all_to_all.15.back_ref = bf16[64,80,256]{2,1,0:T(8,128)(2,1)S(1)} all-to-all(bf16[64,80,256]{2,1,0:T(8,128)(2,1)S(1)} %subtract.1), channel_id=1, replica_groups=mesh['y'=4,'far'=4,'near'=2,'x'=4,'c'=2] {'c','y','x','near'}, dimensions={0} | all-to-all | bytes 5242880 | tf_op jit(solution)/shard_map/all_to_all | solution.py:347
  154.3 1.9 %place.1 = (bf16[64,128,128]{2,1,0:T(8,128)(2,1)}, bf16[16,16384]{1,0:T(8,128)(2,1)}) custom-call(bf16[64,80,256]{2,1,0:T(8,128)(2,1)S(1)} %all_to_all.15.back_ref), custom_call_target="tpu_custom_call" | custom-call | bytes 4194304 | tf_op jit(solution)/shard_map/place/pallas_call | solution.py:299
Async XLA Ops:
  2.0 32.4 %all-to-all-start = ((f32[64,8,128]{2,1,0:T(8,128)}), f32[64,8,128]{2,1,0:T(8,128)S(1)}, u32[]{:S(2)}, u32[]{:S(2)}) async-start(f32[64,8,128]{2,1,0:T(8,128)} %make_lines.1), calls=%async_computation | async-start | bytes 524288 | tf_op jit(solution)/shard_map/all_to_all | solution.py:336
  34.5 36.6 %all-to-all-start.1 = ((bf16[64,64,256]{2,1,0:T(8,128)(2,1)}), bf16[64,64,256]{2,1,0:T(8,128)(2,1)S(1)}, u32[]{:S(2)}, u32[]{:S(2)}) async-start(bf16[64,64,256]{2,1,0:T(8,128)(2,1)} %convolve.1), calls=%async_computation.1 | async-start | bytes 4194304 | tf_op jit(solution)/shard_map/all_to_all | solution.py:339
  73.4 9.9 %collective-permute-start = (bf16[272,256]{1,0:T(8,128)(2,1)S(1)}, bf16[272,256]{1,0:T(8,128)(2,1)S(1)}, u32[]{:S(2)}, u32[]{:S(2)}) collective-permute-start(bf16[272,256]{1,0:T(8,128)(2,1)S(1)} %get-tuple-element.11), channel_id=1, source_target_pairs={{0,32},{16,48},{32,0},{48,16},{1,33},{17,49},{33,1},{49,17},{2,34}... | collective-permute-start | bytes 417800 | tf_op jit(solution)/shard_map/ppermute | solution.py:323
  79.6 11.9 %collective-permute-start.1 = (bf16[272,256]{1,0:T(8,128)(2,1)S(1)}, bf16[272,256]{1,0:T(8,128)(2,1)S(1)}, u32[]{:S(2)}, u32[]{:S(2)}) collective-permute-start(bf16[272,256]{1,0:T(8,128)(2,1)S(1)} %get-tuple-element.12), channel_id=1, source_target_pairs={{0,16},{16,32},{32,48},{48,0},{1,17},{17,33},{33,49},{49,1},{2,18}... | collective-permute-start | bytes 417800 | tf_op jit(solution)/shard_map/ppermute | solution.py:323
  80.8 13.7 %collective-permute-start.2 = (bf16[272,256]{1,0:T(8,128)(2,1)S(1)}, bf16[272,256]{1,0:T(8,128)(2,1)S(1)}, u32[]{:S(2)}, u32[]{:S(2)}) collective-permute-start(bf16[272,256]{1,0:T(8,128)(2,1)S(1)} %get-tuple-element.13), channel_id=1, source_target_pairs={{0,48},{16,0},{32,16},{48,32},{1,49},{17,1},{33,17},{49,33},{2,50}... | collective-permute-start | bytes 417800 | tf_op jit(solution)/shard_map/ppermute | solution.py:323
